TPU v7x, 512 devices: a whole 4x8x8 slice. The times are simulated.
512 devices in a mesh: req: 64 (over z, x, core), tp: 8 (over y).
Axes of the slice: x: 4, y: 8, z: 8, core: 2. Of those that a mesh axis runs over, the one named last changes fastest.
Arguments:
- normed_hidden_input: bfloat16 [1024, 2, 8192], P('req', None, 'tp'), may hold values from -6 to 6
- value_matrix: bfloat16 [8192, 1024], P(None, 'tp'), may hold values from -0.0625 to 0.0625
- adapter_down_weight: bfloat16 [8192, 32768], P('tp', 'req'), may hold values from -0.0625 to 0.0625
- adapter_up_weight: bfloat16 [32768, 1024], P('req', 'tp'), may hold values from -0.75 to 0.75
- request_adapter: int32 [1024], P('req'), may hold values from 0 to 511, as said below
- adapter_storage_row: int32 [512], replicated, may hold values from 0 to 511, as said below
- cache_valid_length: int32 [1024], P('req'), may hold values from 2 to 64
- queries: bfloat16 [1024, 2, 8192], P('req', None, 'tp'), may hold values from -9 to 9
- stored_key_cache: bfloat16 [1024, 64, 1024], P('req', None, 'tp'), may hold values from -4 to 4
- stored_value_cache: bfloat16 [1024, 64, 1024], P('req', None, 'tp'), may hold values from -6 to 6
- step_keys: bfloat16 [1024, 2, 1024], P('req', None, 'tp'), may hold values from -6 to 6
Outputs:
- step_values: bfloat16 [1024, 2, 1024], P('req', None, 'tp')
- attention: bfloat16 [1024, 2, 8192], P('req', None, 'tp')
Inputs may be any that keep to these rules, and one draw needn't show every extreme that they name: `request_adapter`: storage row p lies on home device p // 8. Of the 16 requests of one device, at most 2 use adapters stored on one home device; one home device gets exactly 2 from every device. `adapter_storage_row`: A permutation.
All inputs are finite; a program needn't handle non-finite values.
Results may differ from a plain program's by a relative error of at most 0.0053.
Values may be sent and summed in bfloat16 or wider, within the bound.
No kernel may reach another device: no remote copies, remote signals or barrier semaphores. Data moves between devices by JAX's collectives and lax.ppermute only.
A program may use at most 64 MiB of HBM per device.

v0:
```python
import math

import jax
import jax.numpy as jnp
from jax import lax
from jax.sharding import PartitionSpec as P

HEAD_WIDTH = 128
ADAPTER_RANK = 64
QUERY_PER_KEY = 8


def body(
    normed_hidden_input,
    value_matrix,
    adapter_down_weight,
    adapter_up_weight,
    request_adapter,
    adapter_storage_row,
    cache_valid_length,
    queries,
    stored_key_cache,
    stored_value_cache,
    step_keys,
):
    req_local, step_count, width_local = normed_hidden_input.shape
    value_local = value_matrix.shape[1]
    adapter_delta = adapter_up_weight.shape[0] // ADAPTER_RANK
    my_index = lax.axis_index("req")
    total_adapters = adapter_storage_row.shape[0]
    matches = request_adapter[:, None] == jnp.arange(total_adapters, dtype=jnp.int32)[None, :]
    storage = jnp.sum(jnp.where(matches, adapter_storage_row[None, :], 0), axis=1)
    columns_in = lax.all_gather(normed_hidden_input, "tp", axis=2, tiled=True)
    span = columns_in.shape[2]
    product = jnp.dot(
        columns_in.reshape(-1, span), value_matrix, preferred_element_type=jnp.float32
    )
    plain_values = product.reshape(
        jnp.zeros((req_local, step_count, value_local), jnp.float32).shape
    )
    every_row, every_storage = (
        lax.all_gather(normed_hidden_input, "req", axis=0, tiled=True),
        lax.all_gather(storage, "req", axis=0, tiled=True),
    )
    every_slot = jnp.where(
        every_storage // adapter_delta == my_index, every_storage % adapter_delta, -1
    )
    row_count = every_row.shape[0]
    projected = jnp.dot(
        every_row.reshape(row_count * step_count, width_local),
        adapter_down_weight,
        preferred_element_type=jnp.float32,
    )
    projected = projected.reshape(row_count, step_count, adapter_delta, ADAPTER_RANK)
    chosen = (every_slot[:, None] == jnp.arange(adapter_delta, dtype=jnp.int32)[None, :]).astype(
        jnp.float32
    )
    partial_value = jnp.einsum("nsar,na->nsr", projected, chosen)
    summed_all = lax.psum(partial_value, "tp").astype(jnp.bfloat16)
    row_count = summed_all.shape[0]
    chosen = (
        every_slot[:, None, None, None]
        == jnp.arange(adapter_delta, dtype=jnp.int32)[None, None, :, None]
    )
    spread = jnp.where(chosen, summed_all[:, :, None, :], jnp.zeros((), jnp.bfloat16))
    product = jnp.dot(
        spread.reshape(row_count * step_count, adapter_delta * ADAPTER_RANK),
        adapter_up_weight,
        preferred_element_type=jnp.float32,
    )
    low_rank = lax.psum_scatter(
        product.reshape(row_count, step_count, value_local), "req", scatter_dimension=0, tiled=True
    ).astype(jnp.bfloat16)
    low_rank = lax.optimization_barrier(low_rank)
    step_values = (plain_values + low_rank.astype(jnp.float32)).astype(jnp.bfloat16)
    kv_local = value_local // HEAD_WIDTH
    scale = 1.0 / math.sqrt(HEAD_WIDTH)
    query_head_view = queries.reshape(req_local, step_count, kv_local, QUERY_PER_KEY, HEAD_WIDTH)
    key_head_view = stored_key_cache.reshape(req_local, -1, kv_local, HEAD_WIDTH)
    value_view = stored_value_cache.reshape(req_local, -1, kv_local, HEAD_WIDTH)
    current_keys = step_keys.reshape(req_local, step_count, kv_local, HEAD_WIDTH)
    fresh_values = step_values.reshape(req_local, step_count, kv_local, HEAD_WIDTH)
    context = key_head_view.shape[1]
    cache_scores = (
        jnp.einsum(
            "rskgd,rckd->rskgc", query_head_view, key_head_view, preferred_element_type=jnp.float32
        )
        * scale
    )
    fresh_scores = (
        jnp.einsum(
            "rskgd,rtkd->rskgt", query_head_view, current_keys, preferred_element_type=jnp.float32
        )
        * scale
    )
    valid = jnp.arange(context, dtype=jnp.int32)[None, :] < cache_valid_length[:, None]
    causal = (
        jnp.arange(step_count, dtype=jnp.int32)[None, :]
        <= jnp.arange(step_count, dtype=jnp.int32)[:, None]
    )
    cache_scores = jnp.where(valid[:, None, None, None, :], cache_scores, -jnp.inf)
    fresh_scores = jnp.where(causal[None, :, None, None, :], fresh_scores, -jnp.inf)
    peak = jnp.maximum(jnp.max(cache_scores, axis=-1), jnp.max(fresh_scores, axis=-1))[..., None]
    cache_expo = jnp.exp(cache_scores - peak)
    fresh_expo = jnp.exp(fresh_scores - peak)
    denominator = jnp.sum(cache_expo, axis=-1, keepdims=True) + jnp.sum(
        fresh_expo, axis=-1, keepdims=True
    )
    cache_weights = (cache_expo / denominator).astype(jnp.bfloat16)
    fresh_weights = (fresh_expo / denominator).astype(jnp.bfloat16)
    attended = jnp.einsum(
        "rskgc,rckd->rskgd", cache_weights, value_view, preferred_element_type=jnp.float32
    )
    attended = attended + jnp.einsum(
        "rskgt,rtkd->rskgd", fresh_weights, fresh_values, preferred_element_type=jnp.float32
    )
    attention = attended.astype(jnp.bfloat16).reshape(
        req_local, step_count, kv_local * QUERY_PER_KEY * HEAD_WIDTH
    )
    return (step_values, attention)


def solution(mesh):
    placed = (
        P("req", None, "tp"),
        P(None, "tp"),
        P("tp", "req"),
        P("req", "tp"),
        P("req"),
        P(),
        P("req"),
        P("req", None, "tp"),
        P("req", None, "tp"),
        P("req", None, "tp"),
        P("req", None, "tp"),
    )
    return jax.shard_map(
        body,
        mesh=mesh,
        in_specs=placed,
        out_specs=(P("req", None, "tp"), P("req", None, "tp")),
        check_vma=False,
    )
```

profile of v0, /device:TPU:1, one launch (start us, length us, event | category | flops | bytes accessed | tf_op | source)
XLA Modules:
  0.0 294.0 jit_solution(1287845142571132430)
XLA Ops:
  7.2 0.7 all-gather.2.cloned.1.call-update
  8.0 1.5 copy.28
  9.5 1.3 dynamic-slice
  11.4 0.2 select_reduce_fusion
  11.6 0.2 dynamic-update-slice
  11.9 23.6 %all-reduce = s32[1024]{0:T(1024)S(1)} all-reduce(s32[1024]{0:T(1024)S(1)} %dynamic-update-slice), channel_id=1, replica_groups=mesh['req'=64,'tp'=8] {'req'}, use_global_device_ids=true, to_apply=%add | all-reduce | flops 1024 | bytes 8192
  35.5 67.0 %all-gather.2.cloned.1.call-done = bf16[1024,2,1024]{2,1,0:T(2,128)(2,1)} async-done(((bf16[16,2,1024]{2,1,0:T(2,128)(2,1)}), bf16[1024,2,1024]{2,1,0:T(2,128)(2,1)}) %all-gather.2.cloned.1.call-update) | async-done | bytes 4194320 | tf_op jit(solution)/shard_map/all_gather | solution.py:42
  102.4 5.5 %multiply_reduce_fusion = f32[1024,2,64]{0,2,1:T(8,128)} fusion(bf16[8,64,1024,1]{2,1,0,3:T(8,128)(2,1)S(1)} %bitcast.84, bf16[1024,2,1024,1]{2,1,0,3:T(2,128)(2,1)} %bitcast.86, f32[1024,8]{0,1:T(8,128)S(1)} %get-tuple-element.10), kind=kOutput, calls=%fused_computation.2 | convolution fusion | flops 2149449728 | bytes 5799936 | tf_op jit(solution)/shard_map/dot_general | solution.py:49
  108.0 28.9 %all-reduce.2 = bf16[1024,2,64]{0,2,1:T(8,128)(2,1)S(1)} all-reduce(f32[1024,2,64]{0,2,1:T(8,128)} %multiply_reduce_fusion), channel_id=1, replica_groups=mesh['req'=64,'tp'=8] {'tp'}, use_global_device_ids=true, to_apply=%region_1.2 | all-reduce | flops 131072 | bytes 786432 | tf_op jit(solution)/shard_map/psum | solution.py:59
  136.9 0.1 broadcast_in_dim.83
  137.0 0.3 bitcast_select_fusion
  137.4 1.7 fusion.22
  139.4 0.4 fusion.39
  139.8 0.3 fusion.38
  140.2 0.1 fusion.27
  140.3 0.2 fusion.24
  140.5 19.5 %all_gather.9 = bf16[16,2,8192]{2,0,1:T(8,128)(2,1)S(1)} all-gather(bf16[16,2,1024]{2,0,1:T(8,128)(2,1)S(1)} %copy.27), channel_id=1, replica_groups=mesh['req'=64,'tp'=8] {'tp'}, dimensions={2}, use_global_device_ids=true | all-gather | bytes 589824 | tf_op jit(solution)/shard_map/all_gather | solution.py:33
  160.0 124.2 %reduce-scatter.2.cloned.1.call-done = f32[16,2,128]{2,0,1:T(8,128)} async-done(((f32[1024,2,128]{2,0,1:T(8,128)}), f32[16,2,128]{2,0,1:T(8,128)}) %reduce-scatter.2.cloned.1.call-update) | async-done | bytes 16400 | tf_op jit(solution)/shard_map/reduce_scatter | solution.py:71
  284.2 0.7 convert_element_type.29
  284.9 0.4 fusion.16
  285.4 0.6 copy.32
  286.0 0.2 fusion.28
  286.2 0.3 fusion.11
  286.5 0.7 reshape.157
  (32 shorter events, 0.4 us)
Async XLA Ops:
  7.2 277.8 %copy-start = (bf16[8192,128]{1,0:T(8,128)(2,1)S(1)}, bf16[8192,128]{1,0:T(8,128)(2,1)}, u32[]{:S(2)}) copy-start(bf16[8192,128]{1,0:T(8,128)(2,1)} %param.12) | copy-start | bytes 6291460
  7.2 4.2 %copy-start.7 = (s32[16]{0:T(128)S(1)}, s32[16]{0:T(128)}, u32[]{:S(2)}) copy-start(s32[16]{0:T(128)} %param.15) | copy-start | bytes 196
  7.2 4.2 %copy-start.5 = (s32[512]{0:T(512)S(1)}, s32[512]{0:T(512)}, u32[]{:S(2)}) copy-start(s32[512]{0:T(512)} %param.16) | copy-start | bytes 6148
  7.2 95.2 %all-gather.2.cloned.1.call-start = ((), (), s32[]{:S(2)}) async-start(), calls=%async_computation.1 | async-start | bytes 4259840 | tf_op jit(solution)/shard_map/all_gather | solution.py:42
  7.9 276.3 %reduce-scatter.2.cloned.1.call-start = ((), (), s32[]{:S(2)}) async-start(), calls=%async_computation.2 | async-start | bytes 1064960 | tf_op jit(solution)/shard_map/reduce_scatter | solution.py:71
  108.0 29.4 %copy-start.3 = (bf16[512,128]{1,0:T(8,128)(2,1)S(1)}, bf16[512,128]{1,0:T(8,128)(2,1)}, u32[]{:S(2)}) copy-start(bf16[512,128]{1,0:T(8,128)(2,1)} %param.14) | copy-start | bytes 393220
  137.4 1.8 copy-start.2
  137.4 1.9 copy-start.4
  137.4 1.9 copy-start.6
  137.4 2.0 copy-start.9
  137.4 2.4 copy-start.1
  140.1 146.1 %copy-start.8 = (bf16[16,64,128]{2,1,0:T(8,128)(2,1)S(1)}, bf16[16,64,128]{2,1,0:T(8,128)(2,1)}, u32[]{:S(2)}) copy-start(bf16[16,64,128]{2,1,0:T(8,128)(2,1)} %param.20) | copy-start | bytes 786436
Sparse Core Ops, SparseCore 0:
  11.4 91.0 all-gather.1
  139.3 144.8 reduce-scatter.1
where the time goes:
time: 298 us; the launch traced here: 294 us
  waiting for transfers between devices  192 us (64%)
  blocking collectives  72 us (24%)
  between operations  14.9 us (5%)
  matrix products  8.95 us (3%)
  local copies, waits for them, and re-layouts  4.54 us (2%)
    reduce_scatter x1, waiting for transfers between devices, body(): lax.psum_scatter(product.reshape(row_count, step_count, value_local), 're...  124 us
    all_gather x1, waiting for transfers between devices, body(): lax.all_gather(normed_hidden_input, 'req', axis=0, tiled=True)  67 us
    psum x1, blocking collectives, body(): summed_all = lax.psum(partial_value, 'tp').astype(jnp.bfloat16)  28.9 us
    unnamed x1, blocking collectives  23.6 us
    all_gather x1, blocking collectives, body(): columns_in = lax.all_gather(normed_hidden_input, 'tp', axis=2, tiled=True)  19.5 us
  transfers between devices with their start and end apart: 2, of which 2 were waited for; matrix products, arithmetic and copies ran while one was open for 2% of the time, Pallas kernels for 0%

commit v1 on v0

v1 whole, which is shorter than its diff:
```python
import math

import jax
import jax.numpy as jnp
from jax import lax
from jax.sharding import PartitionSpec as P

HEAD_WIDTH = 128
ADAPTER_RANK = 64
QUERY_PER_KEY = 8
CAP = 2
BF = jnp.bfloat16
F32 = jnp.float32


def body(
    normed_hidden_input,
    value_matrix,
    adapter_down_weight,
    adapter_up_weight,
    request_adapter,
    adapter_storage_row,
    cache_valid_length,
    queries,
    stored_key_cache,
    stored_value_cache,
    step_keys,
):
    x = normed_hidden_input
    R, S, W = x.shape
    V = value_matrix.shape[1]
    A = adapter_up_weight.shape[0] // ADAPTER_RANK
    H = lax.axis_size("req")
    T = lax.axis_size("tp")
    total_adapters = adapter_storage_row.shape[0]
    matches = request_adapter[:, None] == jnp.arange(total_adapters, dtype=jnp.int32)[None, :]
    storage = jnp.sum(jnp.where(matches, adapter_storage_row[None, :], 0), axis=1)
    home = storage // A
    slot = storage % A
    same = (home[:, None] == home[None, :]) & (jnp.arange(R)[None, :] < jnp.arange(R)[:, None])
    place = home * CAP + jnp.sum(same.astype(jnp.int32), axis=1)
    pick = (place[None, :] == jnp.arange(H * CAP, dtype=jnp.int32)[:, None]).astype(BF)
    code = jnp.broadcast_to(slot.astype(BF)[:, None, None], (R, S, 128))
    outgoing = jnp.einsum(
        "ki,isd->ksd", pick, jnp.concatenate([x, code], axis=2), preferred_element_type=F32
    ).astype(BF)
    arrived = lax.all_to_all(outgoing.reshape(H, CAP * S, W + 128), "req", 0, 0)
    arrived = arrived.reshape(H * CAP * S, W + 128)
    rows = H * CAP * S
    row_slot = arrived[:, W].astype(jnp.int32)
    projected = jnp.dot(arrived[:, :W], adapter_down_weight, preferred_element_type=F32)
    chosen = row_slot[:, None] == jnp.arange(A, dtype=jnp.int32)[None, :]
    partial = jnp.sum(
        jnp.where(chosen[:, :, None], projected.reshape(rows, A, ADAPTER_RANK), 0.0), axis=1
    )
    partial = jnp.concatenate([partial[: rows // 2], partial[rows // 2 :]], axis=1)
    high = partial.astype(BF)
    low = (partial - high.astype(F32)).astype(BF)
    message = jnp.concatenate(
        [high, low] + [x[:, s, c * 128 : (c + 1) * 128] for s in range(S) for c in range(W // 128)],
        axis=0,
    )
    message = jnp.broadcast_to(message[None], (T,) + message.shape)
    message = lax.all_to_all(message, "tp", 0, 0)
    half = rows // 2
    summed = jnp.sum(
        message[:, :half].astype(F32) + message[:, half : 2 * half].astype(F32), axis=0
    ).astype(BF)
    summed = jnp.concatenate([summed[:, :ADAPTER_RANK], summed[:, ADAPTER_RANK:]], axis=0)
    spread = jnp.where(chosen[:, :, None], summed[:, None, :], jnp.zeros((), BF))
    back = jnp.dot(
        spread.reshape(rows, A * ADAPTER_RANK), adapter_up_weight, preferred_element_type=F32
    ).astype(BF)
    back = lax.all_to_all(back.reshape(H, CAP * S, V), "req", 0, 0)
    low_rank = jnp.einsum(
        "ki,ksd->isd", pick, back.reshape(H * CAP, S, V), preferred_element_type=F32
    ).reshape(R, S, V)
    full = message[:, 2 * half :].reshape(T, S, W // 128, R, 128)
    base = jnp.einsum(
        "tscrl,tclv->rsv",
        full,
        value_matrix.reshape(T, W // 128, 128, V),
        preferred_element_type=F32,
    )
    step_values = (base + low_rank).astype(BF)

    kv_local = V // HEAD_WIDTH
    scale = 1.0 / math.sqrt(HEAD_WIDTH)
    query_head_view = queries.reshape(R, S, kv_local, QUERY_PER_KEY, HEAD_WIDTH)
    key_head_view = stored_key_cache.reshape(R, -1, kv_local, HEAD_WIDTH)
    value_view = stored_value_cache.reshape(R, -1, kv_local, HEAD_WIDTH)
    current_keys = step_keys.reshape(R, S, kv_local, HEAD_WIDTH)
    fresh_values = step_values.reshape(R, S, kv_local, HEAD_WIDTH)
    context = key_head_view.shape[1]
    cache_scores = (
        jnp.einsum("rskgd,rckd->rskgc", query_head_view, key_head_view, preferred_element_type=F32)
        * scale
    )
    fresh_scores = (
        jnp.einsum("rskgd,rtkd->rskgt", query_head_view, current_keys, preferred_element_type=F32)
        * scale
    )
    valid = jnp.arange(context, dtype=jnp.int32)[None, :] < cache_valid_length[:, None]
    causal = (
        jnp.arange(S, dtype=jnp.int32)[None, :] <= jnp.arange(S, dtype=jnp.int32)[:, None]
    )
    cache_scores = jnp.where(valid[:, None, None, None, :], cache_scores, -jnp.inf)
    fresh_scores = jnp.where(causal[None, :, None, None, :], fresh_scores, -jnp.inf)
    peak = jnp.maximum(jnp.max(cache_scores, axis=-1), jnp.max(fresh_scores, axis=-1))[..., None]
    cache_expo = jnp.exp(cache_scores - peak)
    fresh_expo = jnp.exp(fresh_scores - peak)
    denominator = jnp.sum(cache_expo, axis=-1, keepdims=True) + jnp.sum(
        fresh_expo, axis=-1, keepdims=True
    )
    cache_weights = (cache_expo / denominator).astype(BF)
    fresh_weights = (fresh_expo / denominator).astype(BF)
    attended = jnp.einsum(
        "rskgc,rckd->rskgd", cache_weights, value_view, preferred_element_type=F32
    )
    attended = attended + jnp.einsum(
        "rskgt,rtkd->rskgd", fresh_weights, fresh_values, preferred_element_type=F32
    )
    attention = attended.astype(BF).reshape(R, S, kv_local * QUERY_PER_KEY * HEAD_WIDTH)
    return (step_values, attention)


def solution(mesh):
    placed = (
        P("req", None, "tp"),
        P(None, "tp"),
        P("tp", "req"),
        P("req", "tp"),
        P("req"),
        P(),
        P("req"),
        P("req", None, "tp"),
        P("req", None, "tp"),
        P("req", None, "tp"),
        P("req", None, "tp"),
    )
    return jax.shard_map(
        body,
        mesh=mesh,
        in_specs=placed,
        out_specs=(P("req", None, "tp"), P("req", None, "tp")),
        check_vma=False,
    )
```

time: 298 us -> 99.5 us (0.33); the launches traced: 294 us -> 99 us
  waiting for transfers between devices: 192 us -> 46.8 us
  blocking collectives: 72 us -> 0 us
  starting transfers between devices: 0.08 us -> 27.1 us
  between operations: 14.9 us -> 1.07 us
  local copies, waits for them, and re-layouts: 4.54 us -> 13.4 us
    reduce_scatter x1 -> x0, waiting for transfers between devices: 124 us -> none  [body(): lax.psum_scatter(product.reshape(row_count, step_count, value_local), 're...]
    all_gather x1 -> x0, waiting for transfers between devices: 67 us -> none  [body(): lax.all_gather(normed_hidden_input, 'req', axis=0, tiled=True)]
    all_to_all x0 -> x3, waiting for transfers between devices: none -> 46.8 us  [the longest x1 24.9 us: body(): message = lax.all_to_all(message, 'tp', 0, 0)]
    psum x1 -> x0, blocking collectives: 28.9 us -> none  [body(): summed_all = lax.psum(partial_value, 'tp').astype(jnp.bfloat16)]
    all_to_all x0 -> x3, starting transfers between devices: none -> 27.1 us  [the longest x1 14.8 us: body(): arrived = lax.all_to_all(outgoing.reshape(H, CAP * S, W + 128), 'req', 0, 0)]
    unnamed x1 -> x0, blocking collectives: 23.6 us -> none
    all_gather x1 -> x0, blocking collectives: 19.5 us -> none  [body(): columns_in = lax.all_gather(normed_hidden_input, 'tp', axis=2, tiled=True)]
    squeeze x0 -> x17, local copies, waits for them, and re-layouts: none -> 6.68 us  [body(): x[:, s, c * 128:(c + 1) * 128]]
  transfers between devices with their start and end apart: 2 -> 3, of which waited for: 2 -> 3; matrix products, arithmetic and copies ran while one was open for 2% -> 12% of each run, Pallas kernels for 0% -> 0%
where the time goes in v1:
time: 99.5 us; the launch traced here: 99 us
  waiting for transfers between devices  46.8 us (47%)
  starting transfers between devices  27.1 us (27%)
  local copies, waits for them, and re-layouts  13.4 us (13%)
  matrix products  7.41 us (7%)
  other arithmetic  3.17 us (3%)
  between operations  1.07 us (1%)
    all_to_all x1, waiting for transfers between devices, body(): message = lax.all_to_all(message, 'tp', 0, 0)  24.9 us
    all_to_all x1, starting transfers between devices, body(): arrived = lax.all_to_all(outgoing.reshape(H, CAP * S, W + 128), 'req', 0, 0)  14.8 us
    all_to_all x1, waiting for transfers between devices, body(): arrived = lax.all_to_all(outgoing.reshape(H, CAP * S, W + 128), 'req', 0, 0)  12.3 us
    all_to_all x1, waiting for transfers between devices, body(): back = lax.all_to_all(back.reshape(H, CAP * S, V), 'req', 0, 0)  9.57 us
    all_to_all x1, starting transfers between devices, body(): message = lax.all_to_all(message, 'tp', 0, 0)  6.82 us
    squeeze x17, local copies, waits for them, and re-layouts, body(): x[:, s, c * 128:(c + 1) * 128]  6.68 us
    all_to_all x1, starting transfers between devices, body(): back = lax.all_to_all(back.reshape(H, CAP * S, V), 'req', 0, 0)  5.47 us
  transfers between devices with their start and end apart: 3, of which 3 were waited for; matrix products, arithmetic and copies ran while one was open for 12% of the time, Pallas kernels for 0%

profile of v1, /device:TPU:1, one launch (start us, length us, event | category | flops | bytes accessed | tf_op | source)
XLA Modules:
  0.0 99.0 jit_solution(17151792013583258224)
XLA Ops:
  0.6 1.0 %select_reduce_fusion.1 = s32[16]{0:T(128)S(1)} fusion(s32[512]{0:T(512)} %param.16, s32[16]{0:T(128)} %param.15), kind=kLoop, calls=%fused_computation.38 | loop fusion | flops 24560 | bytes 2176 | tf_op jit(solution)/shard_map/reduce_sum | solution.py:37
  1.9 0.9 copy.83
  3.9 1.0 %reshape.216 = bf16[64,4,1152]{2,1,0:T(4,128)(2,1)} reshape(bf16[128,2,1152]{2,1,0:T(2,128)(2,1)S(1)} %copy.84) | data formatting | bytes 1179648 | tf_op jit(solution)/shard_map/reshape | solution.py:47
  4.9 14.8 %all-to-all-start = ((bf16[64,4,1152]{2,1,0:T(4,128)(2,1)}), bf16[64,4,1152]{2,1,0:T(4,128)(2,1)S(1)}, u32[]{:S(2)}, u32[]{:S(2)}) async-start(bf16[64,4,1152]{2,1,0:T(4,128)(2,1)} %reshape.216), calls=%async_computation | async-start | bytes 1179648 | tf_op jit(solution)/shard_map/all_to_all | solution.py:47
  20.8 0.7 copy.111
  21.5 0.7 copy.112
  22.9 0.7 copy.114
  23.6 0.7 copy.115
  24.3 0.7 copy.116
  25.0 0.7 copy.117
  25.8 0.7 copy.118
  26.5 12.3 %all-to-all-done = bf16[64,4,1152]{2,1,0:T(4,128)(2,1)S(1)} async-done(((bf16[64,4,1152]{2,1,0:T(4,128)(2,1)}), bf16[64,4,1152]{2,1,0:T(4,128)(2,1)S(1)}, u32[]{:S(2)}, u32[]{:S(2)}) %all-to-all-start) | async-done | bytes 589856 | tf_op jit(solution)/shard_map/all_to_all | solution.py:47
  39.1 1.8 %fusion.9 = f32[256,512]{0,1:T(8,128)S(1)} fusion(bf16[1024,512]{1,0:T(8,128)(2,1)} %param.13, bf16[256,1152]{1,0:T(8,128)(2,1)S(1)} %reshape.217), kind=kOutput, calls=%fused_computation.16 | convolution fusion | flops 268435456 | bytes 2097152 | tf_op jit(solution)/shard_map/dot_general | solution.py:51
  41.5 1.1 %broadcast_in_dim.75 = bf16[8,512,128]{2,1,0:T(8,128)(2,1)} broadcast(bf16[512,128]{1,0:T(8,128)(2,1)S(1)} %copy.119), dimensions={1,2} | broadcast | bytes 1179648 | tf_op jit(solution)/shard_map/broadcast_in_dim | solution.py:63
  42.6 6.8 %all-to-all-start.1 = ((bf16[8,512,128]{2,1,0:T(8,128)(2,1)}), bf16[8,512,128]{2,1,0:T(8,128)(2,1)S(1)}, u32[]{:S(2)}, u32[]{:S(2)}) async-start(bf16[8,512,128]{2,1,0:T(8,128)(2,1)} %broadcast_in_dim.75), calls=%async_computation.1 | async-start | bytes 2097152 | tf_op jit(solution)/shard_map/all_to_all | solution.py:64
  49.4 0.9 reshape.223
  50.3 0.7 iota_compare_fusion.1
  51.1 1.1 %fusion.38 = (f32[16,2,8]{2,1,0:T(2,128)S(1)}, f32[16,2,1,8,2]{3,4,1,0,2:T(2,128)S(1)}) fusion(bf16[16,2,8,128]{3,2,1,0:T(8,128)(2,1)S(1)} %reshape.223, bf16[16,2,128]{2,1,0:T(2,128)(2,1)} %param.21, pred[2,2]{1,0:T(4,128)(4,1)S(1)} %iota_compare_fusion.5), kind=kOutput, calls=%fused_computation.84 | convolution fusion | flops 132352 | bytes 76804 | tf_op jit(solution)/shard_map/rskgd,rtkd->rskgt/dot_general | solution.py:100
  52.2 1.2 %fusion.37 = (f32[16,2,8]{2,1,0:T(2,128)S(1)}, f32[16,2,1,8,64]{4,3,1,0,2:T(8,128)S(1)}) fusion(bf16[16,2,8,128]{3,2,1,0:T(8,128)(2,1)} %copy-done.2, bf16[16,64,128]{2,1,0:T(8,128)(2,1)S(1)} %copy-done.1, pred[16,64]{1,0:T(8,128)(4,1)S(1)} %iota_compare_fusion.1), kind=kOutput, calls=%fused_computation.83 | convolution fusion | flops 4243200 | bytes 395264 | tf_op jit(solution)/shard_map/rskgd,rckd->rskgc/dot_general | solution.py:96
  53.7 24.9 %all-to-all-done.1 = bf16[8,512,128]{2,1,0:T(8,128)(2,1)S(1)} async-done(((bf16[8,512,128]{2,1,0:T(8,128)(2,1)}), bf16[8,512,128]{2,1,0:T(8,128)(2,1)S(1)}, u32[]{:S(2)}, u32[]{:S(2)}) %all-to-all-start.1) | async-done | bytes 1048608 | tf_op jit(solution)/shard_map/all_to_all | solution.py:64
  78.9 0.7 broadcast_select_fusion
  79.6 1.8 %convolution_convert_fusion.1 = bf16[256,128]{1,0:T(8,128)(2,1)} fusion(bf16[256,512]{0,1:T(8,128)(2,1)S(1)} %bitcast.119, bf16[512,128]{1,0:T(8,128)(2,1)} %param.14), kind=kOutput, calls=%fused_computation.6 | convolution fusion | flops 33587200 | bytes 458752 | tf_op jit(solution)/shard_map/dot_general | solution.py:71
  81.5 5.5 %all-to-all-start.2 = ((bf16[64,4,128]{2,1,0:T(4,128)(2,1)}), bf16[64,4,128]{2,1,0:T(4,128)(2,1)S(1)}, u32[]{:S(2)}, u32[]{:S(2)}) async-start(bf16[64,4,128]{2,1,0:T(4,128)(2,1)} %bitcast.27), calls=%async_computation.2 | async-start | bytes 131072 | tf_op jit(solution)/shard_map/all_to_all | solution.py:74
  87.5 9.6 %all-to-all-done.2 = bf16[64,4,128]{2,1,0:T(4,128)(2,1)S(1)} async-done(((bf16[64,4,128]{2,1,0:T(4,128)(2,1)}), bf16[64,4,128]{2,1,0:T(4,128)(2,1)S(1)}, u32[]{:S(2)}, u32[]{:S(2)}) %all-to-all-start.2) | async-done | bytes 65568 | tf_op jit(solution)/shard_map/all_to_all | solution.py:74
  (76 shorter events, 6.8 us)
Async XLA Ops:
  0.6 86.4 %copy-start = (bf16[8192,128]{1,0:T(8,128)(2,1)S(1)}, bf16[8192,128]{1,0:T(8,128)(2,1)}, u32[]{:S(2)}) copy-start(bf16[8192,128]{1,0:T(8,128)(2,1)} %param.12) | copy-start | bytes 6291460
  1.9 0.9 copy-start.14
  4.9 33.9 %all-to-all-start = ((bf16[64,4,1152]{2,1,0:T(4,128)(2,1)}), bf16[64,4,1152]{2,1,0:T(4,128)(2,1)S(1)}, u32[]{:S(2)}, u32[]{:S(2)}) async-start(bf16[64,4,1152]{2,1,0:T(4,128)(2,1)} %reshape.216), calls=%async_computation | async-start | bytes 1179648 | tf_op jit(solution)/shard_map/all_to_all | solution.py:47
  38.9 2.1 %copy-start.3 = (bf16[16,128]{0,1:T(8,128)(2,1)S(1)}, bf16[16,128]{0,1:T(8,128)(2,1)}, u32[]{:S(2)}) copy-start(bf16[16,128]{0,1:T(8,128)(2,1)} %copy.111) | copy-start | bytes 12292
  38.9 2.1 %copy-start.4 = (bf16[16,128]{0,1:T(8,128)(2,1)S(1)}, bf16[16,128]{0,1:T(8,128)(2,1)}, u32[]{:S(2)}) copy-start(bf16[16,128]{0,1:T(8,128)(2,1)} %copy.112) | copy-start | bytes 12292
  39.0 2.1 %copy-start.5 = (bf16[16,128]{0,1:T(8,128)(2,1)S(1)}, bf16[16,128]{0,1:T(8,128)(2,1)}, u32[]{:S(2)}) copy-start(bf16[16,128]{0,1:T(8,128)(2,1)} %copy.113) | copy-start | bytes 12292
  39.0 2.1 %copy-start.6 = (bf16[16,128]{0,1:T(8,128)(2,1)S(1)}, bf16[16,128]{0,1:T(8,128)(2,1)}, u32[]{:S(2)}) copy-start(bf16[16,128]{0,1:T(8,128)(2,1)} %copy.114) | copy-start | bytes 12292
  39.0 2.1 %copy-start.7 = (bf16[16,128]{0,1:T(8,128)(2,1)S(1)}, bf16[16,128]{0,1:T(8,128)(2,1)}, u32[]{:S(2)}) copy-start(bf16[16,128]{0,1:T(8,128)(2,1)} %copy.115) | copy-start | bytes 12292
  39.0 2.1 %copy-start.8 = (bf16[16,128]{0,1:T(8,128)(2,1)S(1)}, bf16[16,128]{0,1:T(8,128)(2,1)}, u32[]{:S(2)}) copy-start(bf16[16,128]{0,1:T(8,128)(2,1)} %copy.116) | copy-start | bytes 12292
  39.0 2.1 %copy-start.9 = (bf16[16,128]{0,1:T(8,128)(2,1)S(1)}, bf16[16,128]{0,1:T(8,128)(2,1)}, u32[]{:S(2)}) copy-start(bf16[16,128]{0,1:T(8,128)(2,1)} %copy.117) | copy-start | bytes 12292
  39.0 2.1 %copy-start.10 = (bf16[16,128]{0,1:T(8,128)(2,1)S(1)}, bf16[16,128]{0,1:T(8,128)(2,1)}, u32[]{:S(2)}) copy-start(bf16[16,128]{0,1:T(8,128)(2,1)} %copy.118) | copy-start | bytes 12292
  39.1 3.5 %copy-start.13 = (pred[256,8]{0,1:T(8,128)(4,1)}, pred[256,8]{0,1:T(8,128)(4,1)S(1)}, u32[]{:S(2)}) copy-start(pred[256,8]{0,1:T(8,128)(4,1)S(1)} %iota_compare_fusion.2) | copy-start | bytes 6148
  41.3 10.9 %copy-start.1 = (bf16[16,64,128]{2,1,0:T(8,128)(2,1)S(1)}, bf16[16,64,128]{2,1,0:T(8,128)(2,1)}, u32[]{:S(2)}) copy-start(bf16[16,64,128]{2,1,0:T(8,128)(2,1)} %param.19) | copy-start | bytes 786436
  42.6 36.1 %all-to-all-start.1 = ((bf16[8,512,128]{2,1,0:T(8,128)(2,1)}), bf16[8,512,128]{2,1,0:T(8,128)(2,1)S(1)}, u32[]{:S(2)}, u32[]{:S(2)}) async-start(bf16[8,512,128]{2,1,0:T(8,128)(2,1)} %broadcast_in_dim.75), calls=%async_computation.1 | async-start | bytes 2097152 | tf_op jit(solution)/shard_map/all_to_all | solution.py:64
  50.3 0.8 copy-start.2
  52.2 1.5 %copy-start.11 = (f32[16,2,1,8,2]{3,4,1,0,2:T(2,128)}, f32[16,2,1,8,2]{3,4,1,0,2:T(2,128)S(1)}, u32[]{:S(2)}) copy-start(f32[16,2,1,8,2]{3,4,1,0,2:T(2,128)S(1)} %get-tuple-element.35) | copy-start | bytes 6148
  79.6 17.4 %copy-start.15 = (s32[16]{0:T(128)S(1)}, s32[16]{0:T(128)}, u32[]{:S(2)}) copy-start(s32[16]{0:T(128)} %copy-done.14) | copy-start | bytes 196
  79.6 18.2 %copy-start.12 = (f32[16,2,1,8,2]{3,4,1,0,2:T(2,128)S(1)}, f32[16,2,1,8,2]{3,4,1,0,2:T(2,128)}, u32[]{:S(2)}) copy-start(f32[16,2,1,8,2]{3,4,1,0,2:T(2,128)} %copy-done.11) | copy-start | bytes 6148
  81.5 15.6 %all-to-all-start.2 = ((bf16[64,4,128]{2,1,0:T(4,128)(2,1)}), bf16[64,4,128]{2,1,0:T(4,128)(2,1)S(1)}, u32[]{:S(2)}, u32[]{:S(2)}) async-start(bf16[64,4,128]{2,1,0:T(4,128)(2,1)} %bitcast.27), calls=%async_computation.2 | async-start | bytes 131072 | tf_op jit(solution)/shard_map/all_to_all | solution.py:74
  87.0 11.1 %copy-start.16 = (bf16[16,64,128]{2,1,0:T(8,128)(2,1)S(1)}, bf16[16,64,128]{2,1,0:T(8,128)(2,1)}, u32[]{:S(2)}) copy-start(bf16[16,64,128]{2,1,0:T(8,128)(2,1)} %param.20) | copy-start | bytes 786436

commit v2 on v1

v2 whole, which is shorter than its diff:
```python
import functools
import math

import jax
import jax.numpy as jnp
from jax import lax
from jax.experimental import pallas as pl
from jax.experimental.pallas import tpu as pltpu
from jax.sharding import PartitionSpec as P

HEAD_WIDTH = 128
ADAPTER_RANK = 64
QUERY_PER_KEY = 8
CAP = 2
LANES = 128
BF = jnp.bfloat16
F32 = jnp.float32
I32 = jnp.int32


def iota(shape, dim):
    return lax.broadcasted_iota(I32, shape, dim)


def dot(a, b):
    return jnp.dot(a, b, preferred_element_type=F32)


def picker(place_ref, rows, steps, requests):
    shape = (rows, requests * steps)
    column = iota((1, requests * steps), 1)
    target = jnp.zeros((1, requests * steps), I32)
    for i in range(requests):
        target = jnp.where(column // steps == i, place_ref[i] * steps + column % steps, target)
    return jnp.where(iota(shape, 0) == target, 1.0, 0.0).astype(BF)


def route_kernel(adapters, adapter_ref, storage_ref, x_ref, send_ref, wide_ref, place_ref):
    requests, steps, width = x_ref.shape
    homes = send_ref.shape[0]
    rows = homes * CAP * steps
    storage = [storage_ref[adapter_ref[i]] for i in range(requests)]
    home = [s // adapters for s in storage]
    code = jnp.zeros((requests * steps, LANES), I32)
    row = iota((requests * steps, LANES), 0)
    for i in range(requests):
        earlier = jnp.int32(0)
        for k in range(i):
            earlier = earlier + (home[k] == home[i]).astype(I32)
        place_ref[i] = home[i] * CAP + earlier
        code = jnp.where(row // steps == i, storage[i] % adapters, code)
    x = x_ref[...].reshape(requests * steps, width)
    wide_ref[...] = x.astype(F32)
    pick = picker(place_ref, rows, steps, requests)
    send = dot(pick, jnp.concatenate([x, code.astype(F32).astype(BF)], axis=1))
    send_ref[...] = send.astype(BF).reshape(send_ref.shape)


def down_kernel(halves, seen_ref, down_ref, part_ref, code_ref):
    homes, per, width = seen_ref.shape
    width = width - LANES
    seen = seen_ref[...].reshape(homes * per, width + LANES)
    code = seen[:, width:].astype(F32)
    code_ref[...] = code
    product = dot(seen[:, :width], down_ref[...])
    lane = iota(code.shape, 1)
    own = jnp.zeros(code.shape, F32)
    for m in range(product.shape[1] // LANES):
        here = (2 * m + lane // ADAPTER_RANK).astype(F32) == code
        own = jnp.where(here, product[:, m * LANES : (m + 1) * LANES], own)
    own = own + pltpu.roll(own, ADAPTER_RANK, 1)
    half = own.shape[0] // 2
    part = jnp.where(iota((half, LANES), 1) < ADAPTER_RANK, own[:half], own[half:])
    pieces = []
    for _ in range(halves):
        high = part.astype(BF)
        pieces.append(high)
        part = part - high.astype(F32)
    part = jnp.concatenate(pieces, axis=0)
    for t in range(part_ref.shape[0]):
        part_ref[t] = part


def up_kernel(halves, part_ref, code_ref, up_ref, back_ref):
    code = code_ref[...]
    half = code.shape[0] // 2
    total = jnp.zeros((half, LANES), F32)
    for t in range(part_ref.shape[0]):
        for k in range(halves):
            total = total + part_ref[t, k * half : (k + 1) * half].astype(F32)
    total = total.astype(BF).astype(F32)
    turned = pltpu.roll(total, ADAPTER_RANK, 1)
    left = iota((half, LANES), 1) < ADAPTER_RANK
    both = jnp.concatenate(
        [jnp.where(left, total, turned), jnp.where(left, turned, total)], axis=0
    )
    lane = iota(code.shape, 1)
    spread = []
    for m in range(up_ref.shape[0] // LANES):
        here = (2 * m + lane // ADAPTER_RANK).astype(F32) == code
        spread.append(jnp.where(here, both, 0.0).astype(BF))
    back = dot(jnp.concatenate(spread, axis=1), up_ref[...]).astype(BF)
    back_ref[...] = back.reshape(back_ref.shape)


def scores_kernel(length_ref, q_ref, key_ref, value_ref, fresh_ref, part_ref, weight_ref):
    requests, steps, width = q_ref.shape
    context = key_ref.shape[1]
    groups = width // HEAD_WIDTH
    n = requests * steps
    scale = 1.0 / math.sqrt(HEAD_WIDTH)
    q = q_ref[...].reshape(n, width)
    q = jnp.concatenate(
        [q[:, g * HEAD_WIDTH : (g + 1) * HEAD_WIDTH] for g in range(groups)], axis=0
    )
    keys = key_ref[...].reshape(requests * context, HEAD_WIDTH)
    values = value_ref[...].reshape(requests * context, HEAD_WIDTH)
    fresh = fresh_ref[...].reshape(n, HEAD_WIDTH)
    contract = (((1,), (1,)), ((), ()))
    cached = lax.dot_general(q, keys, contract, preferred_element_type=F32) * scale
    new = lax.dot_general(q, fresh, contract, preferred_element_type=F32) * scale
    column = iota((1, requests * context), 1)
    limit = jnp.zeros((1, requests * context), I32)
    for i in range(requests):
        limit = jnp.where(column // context == i, length_ref[i], limit)
    owner = jnp.where(column % context < limit, column // context, -1)
    row = iota((groups * n, 1), 0) % n
    cached = jnp.where(row // steps == owner, cached, -jnp.inf)
    other = iota((1, n), 1)
    new = jnp.where(
        (row // steps == other // steps) & (other % steps <= row % steps), new, -jnp.inf
    )
    peak = jnp.maximum(
        jnp.max(cached, axis=1, keepdims=True), jnp.max(new, axis=1, keepdims=True)
    )
    cached = jnp.exp(cached - peak)
    new = jnp.exp(new - peak)
    total = jnp.sum(cached, axis=1, keepdims=True) + jnp.sum(new, axis=1, keepdims=True)
    weight_ref[...] = (new / total).astype(BF)
    part_ref[...] = dot((cached / total).astype(BF), values)


def base_kernel(wide_ref, value_ref, base_ref):
    width = wide_ref.shape[2]
    total = jnp.zeros(base_ref.shape, F32)
    for t in range(wide_ref.shape[0]):
        total = total + dot(wide_ref[t].astype(BF), value_ref[t * width : (t + 1) * width, :])
    base_ref[...] = total


def finish_kernel(place_ref, back_ref, base_ref, part_ref, weight_ref, step_ref, out_ref):
    requests, steps, width = out_ref.shape
    homes, per, columns = back_ref.shape
    n = requests * steps
    pick = picker(place_ref, homes * per, steps, requests)
    back = back_ref[...].reshape(homes * per, columns)
    low = lax.dot_general(pick, back, (((0,), (0,)), ((), ())), preferred_element_type=F32)
    step = (base_ref[...] + low).astype(BF)
    step_ref[...] = step.reshape(step_ref.shape)
    attended = (part_ref[...] + dot(weight_ref[...], step)).astype(BF)
    attended = jnp.concatenate(
        [attended[g * n : (g + 1) * n] for g in range(width // HEAD_WIDTH)], axis=1
    )
    out_ref[...] = attended.reshape(out_ref.shape)


VM = pl.BlockSpec(memory_space=pltpu.VMEM)
SM = pl.BlockSpec(memory_space=pltpu.SMEM)


def call(kernel, ins, outs, args, flops=0, bytes_accessed=0):
    return pl.pallas_call(
        kernel,
        in_specs=list(ins),
        out_specs=tuple(s for s, _ in outs),
        out_shape=tuple(o for _, o in outs),
        compiler_params=pltpu.CompilerParams(vmem_limit_bytes=32 * 1024 * 1024),
        cost_estimate=pl.CostEstimate(
            flops=flops, bytes_accessed=bytes_accessed, transcendentals=0
        ),
    )(*args)


def body(
    normed_hidden_input,
    value_matrix,
    adapter_down_weight,
    adapter_up_weight,
    request_adapter,
    adapter_storage_row,
    cache_valid_length,
    queries,
    stored_key_cache,
    stored_value_cache,
    step_keys,
):
    x = normed_hidden_input
    R, S, W = x.shape
    V = value_matrix.shape[1]
    A = adapter_up_weight.shape[0] // ADAPTER_RANK
    H = lax.axis_size("req")
    T = lax.axis_size("tp")
    rows = H * CAP * S
    groups = queries.shape[2] // HEAD_WIDTH
    halves = HALVES
    shape = jax.ShapeDtypeStruct
    send, wide, place = call(
        functools.partial(route_kernel, A),
        (SM, SM, VM),
        (
            (VM, shape((H, CAP * S, W + LANES), BF)),
            (VM, shape((R * S, W), F32)),
            (SM, shape((R,), I32)),
        ),
        (request_adapter, adapter_storage_row, x),
    )
    seen = lax.all_to_all(send, "req", 0, 0)
    wide = lax.all_gather(wide, "tp", axis=0)
    attended, weights = call(
        scores_kernel,
        (SM, VM, VM, VM, VM),
        ((VM, shape((groups * R * S, HEAD_WIDTH), F32)), (VM, shape((groups * R * S, R * S), BF))),
        (cache_valid_length, queries, stored_key_cache, stored_value_cache, step_keys),
        flops=10**8,
        bytes_accessed=10**6,
    )
    part, code = call(
        functools.partial(down_kernel, halves),
        (VM, VM),
        ((VM, shape((T, halves * rows // 2, LANES), BF)), (VM, shape((rows, LANES), F32))),
        (seen, adapter_down_weight),
    )
    part = lax.all_to_all(part, "tp", 0, 0)
    part, attended, weights = lax.optimization_barrier((part, attended, weights))
    (back,) = call(
        functools.partial(up_kernel, halves),
        (VM, VM, VM),
        ((VM, shape((H, CAP * S, V), BF)),),
        (part, code, adapter_up_weight),
    )
    back = lax.all_to_all(back, "req", 0, 0)
    (base,) = call(
        base_kernel, (VM, VM), ((VM, shape((R * S, V), F32)),), (wide, value_matrix)
    )
    step_values, attention = call(
        finish_kernel,
        (SM, VM, VM, VM, VM),
        ((VM, shape((R, S, V), BF)), (VM, shape((R, S, groups * HEAD_WIDTH), BF))),
        (place, back, base, attended, weights),
    )
    return (step_values, attention)


HALVES = 2


def solution(mesh):
    placed = (
        P("req", None, "tp"),
        P(None, "tp"),
        P("tp", "req"),
        P("req", "tp"),
        P("req"),
        P(),
        P("req"),
        P("req", None, "tp"),
        P("req", None, "tp"),
        P("req", None, "tp"),
        P("req", None, "tp"),
    )
    return jax.shard_map(
        body,
        mesh=mesh,
        in_specs=placed,
        out_specs=(P("req", None, "tp"), P("req", None, "tp")),
        check_vma=False,
    )
```

time: 99.5 us -> 105 us (1.055)
  between operations: 1.07 us -> 14.2 us
  Pallas kernels: 0 us -> 7.57 us
  matrix products: 7.41 us -> 0 us
  local copies, waits for them, and re-layouts: 13.4 us -> 6.26 us
  starting transfers between devices: 27.1 us -> 31.1 us
  other arithmetic: 3.17 us -> 0 us
  waiting for transfers between devices: 46.8 us -> 45.1 us
    pallas_call x0 -> x6, Pallas kernels: none -> 7.57 us  [call(): pl.pallas_call(kernel, in_specs=list(ins), out_specs=tuple((s for s, _ in...]
    dot_general x9 -> x0, matrix products: 7.41 us -> none  [the longest x1 1.82 us: body(): jnp.dot(spread.reshape(rows, A * ADAPTER_RANK), adapter_up_weight, prefer...]
    squeeze x17 -> x0, local copies, waits for them, and re-layouts: 6.68 us -> none  [body(): x[:, s, c * 128:(c + 1) * 128]]
    unnamed x37 -> x28, local copies, waits for them, and re-layouts: 1.63 us -> 6.26 us
    all_to_all x3, starting transfers between devices: 27.1 us -> 31 us  [the longest x1 15 us: body(): seen = lax.all_to_all(send, 'req', 0, 0)]
    all_to_all x3, waiting for transfers between devices: 46.8 us -> 44.4 us  [the longest x1 18.3 us: body(): seen = lax.all_to_all(send, 'req', 0, 0)]
    reshape x3 -> x0, local copies, waits for them, and re-layouts: 1.83 us -> none  [the longest x1 1.04 us: body(): arrived = lax.all_to_all(outgoing.reshape(H, CAP * S, W + 128), 'req', 0, 0)]
    reduce_sum x6 -> x0, other arithmetic: 1.61 us -> none  [the longest x1 1.02 us: body(): jnp.sum(jnp.where(matches, adapter_storage_row[None, :], 0), axis=1)]
  transfers between devices with their start and end apart: 3 -> 4, of which waited for: 3 -> 3; matrix products, arithmetic and copies ran while one was open for 12% -> 0% of each run, Pallas kernels for 0% -> 4%
where the time goes in v2:
time: 105 us; the launch traced here: 104 us
  waiting for transfers between devices  45.1 us (43%)
  starting transfers between devices  31.1 us (30%)
  between operations  14.2 us (14%)
  Pallas kernels  7.57 us (7%)
  local copies, waits for them, and re-layouts  6.26 us (6%)
    all_to_all x1, waiting for transfers between devices, body(): seen = lax.all_to_all(send, 'req', 0, 0)  18.3 us
    all_to_all x1, waiting for transfers between devices, body(): part = lax.all_to_all(part, 'tp', 0, 0)  17.7 us
    all_to_all x1, starting transfers between devices, body(): seen = lax.all_to_all(send, 'req', 0, 0)  15 us
    all_to_all x1, starting transfers between devices, body(): back = lax.all_to_all(back, 'req', 0, 0)  9.23 us
    all_to_all x1, waiting for transfers between devices, body(): back = lax.all_to_all(back, 'req', 0, 0)  8.39 us
    pallas_call x6, Pallas kernels, call(): pl.pallas_call(kernel, in_specs=list(ins), out_specs=tuple((s for s, _ in...  7.57 us
    all_to_all x1, starting transfers between devices, body(): part = lax.all_to_all(part, 'tp', 0, 0)  6.84 us
    unnamed x28, local copies, waits for them, and re-layouts  6.26 us
  transfers between devices with their start and end apart: 4, of which 3 were waited for; matrix products, arithmetic and copies ran while one was open for 0% of the time, Pallas kernels for 4%

profile of v2, /device:TPU:1, one launch (start us, length us, event | category | flops | bytes accessed | tf_op | source)
XLA Modules:
  0.0 104.2 jit_solution(13127596031672150353)
XLA Ops:
  7.2 0.9 copy-done.8
  8.1 0.7 copy-done.11
  8.8 0.7 copy-done.12
  9.4 1.9 %shard_map.122 = (bf16[64,4,1152]{2,1,0:T(4,128)(2,1)}, f32[32,1024]{1,0:T(8,128)}, s32[16]{0:T(128)S(1)}) custom-call(s32[16]{0:T(128)S(1)} %copy-done.12, s32[512]{0:T(512)S(1)} %copy-done.11, bf16[16,2,1024]{2,1,0:T(2,128)(2,1)S(1)} %copy-done.8), custom_call_target="tpu_custom_call" | custom-call | tf_op jit(solution)/shard_map/pallas_call | solution.py:172
  11.4 0.0 copy-start.5
  11.4 15.0 %all-to-all-start = ((bf16[64,4,1152]{2,1,0:T(4,128)(2,1)}), bf16[64,4,1152]{2,1,0:T(4,128)(2,1)S(1)}, u32[]{:S(2)}, u32[]{:S(2)}) async-start(bf16[64,4,1152]{2,1,0:T(4,128)(2,1)} %get-tuple-element.13), calls=%async_computation | async-start | bytes 1179648 | tf_op jit(solution)/shard_map/all_to_all | solution.py:217
  26.3 0.0 all-gather.3.cloned.1.call-start
  26.4 0.7 all-gather.3.cloned.1.call-update
  27.1 0.0 copy-start
  27.1 18.3 %all-to-all-done.seen_ref = bf16[64,4,1152]{2,1,0:T(4,128)(2,1)S(1)} async-done(((bf16[64,4,1152]{2,1,0:T(4,128)(2,1)}), bf16[64,4,1152]{2,1,0:T(4,128)(2,1)S(1)}, u32[]{:S(2)}, u32[]{:S(2)}) %all-to-all-start) | async-done | bytes 589856 | tf_op jit(solution)/shard_map/all_to_all | solution.py:217
  45.4 1.2 %copy-done.2 = bf16[1024,512]{1,0:T(8,128)(2,1)S(1)} copy-done((bf16[1024,512]{1,0:T(8,128)(2,1)S(1)}, bf16[1024,512]{1,0:T(8,128)(2,1)}, u32[]{:S(2)}) %copy-start.2) | copy-done | bytes 1048600
  46.6 1.3 %shard_map.123 = (bf16[8,256,128]{2,1,0:T(8,128)(2,1)}, f32[256,128]{1,0:T(8,128)S(1)}) custom-call(bf16[64,4,1152]{2,1,0:T(4,128)(2,1)S(1)} %all-to-all-done.seen_ref, bf16[1024,512]{1,0:T(8,128)(2,1)S(1)} %copy-done.2), custom_call_target="tpu_custom_call" | custom-call | tf_op jit(solution)/shard_map/pallas_call | solution.py:172
  48.0 0.7 copy-done.6
  48.6 6.8 %all-to-all-start.1 = ((bf16[8,256,128]{2,1,0:T(8,128)(2,1)}), bf16[8,256,128]{2,1,0:T(8,128)(2,1)S(1)}, u32[]{:S(2)}, u32[]{:S(2)}) async-start(bf16[8,256,128]{2,1,0:T(8,128)(2,1)} %get-tuple-element.14), calls=%async_computation.1 | async-start | bytes 1048576 | tf_op jit(solution)/shard_map/all_to_all | solution.py:233
  55.5 1.4 %shard_map.124 = (f32[256,128]{1,0:T(8,128)S(1)}, bf16[256,32]{1,0:T(8,128)(2,1)S(1)}) custom-call(s32[16]{0:T(128)S(1)} %copy-done.13, bf16[16,2,1024]{2,1,0:T(2,128)(2,1)S(1)} %copy-done.9, bf16[16,64,128]{2,1,0:T(8,128)(2,1)S(1)} %copy-done.3, bf16[16,64,128]{2,1,0:T(8,128)(2,1)S(1)} %copy-done.4, bf16[16,2,128]{2,1,0:T(2,128)(2,1)S(1)} %copy-done.10), custom_call_target="tpu_custom_call" | custom-call | flops 100000000 | bytes 1000000 | tf_op jit(solution)/shard_map/pallas_call | solution.py:172
  56.9 17.7 %all-to-all-done.1.part_ref = bf16[8,256,128]{2,1,0:T(8,128)(2,1)S(1)} async-done(((bf16[8,256,128]{2,1,0:T(8,128)(2,1)}), bf16[8,256,128]{2,1,0:T(8,128)(2,1)S(1)}, u32[]{:S(2)}, u32[]{:S(2)}) %all-to-all-start.1) | async-done | bytes 524320 | tf_op jit(solution)/shard_map/all_to_all | solution.py:233
  74.6 0.9 copy-done.7
  75.5 0.9 shard_map.125
  76.5 9.2 %all-to-all-start.2 = ((bf16[64,4,128]{2,1,0:T(4,128)(2,1)}), bf16[64,4,128]{2,1,0:T(4,128)(2,1)S(1)}, u32[]{:S(2)}, u32[]{:S(2)}) async-start(bf16[64,4,128]{2,1,0:T(4,128)(2,1)} %shard_map.125), calls=%async_computation.2 | async-start | bytes 131072 | tf_op jit(solution)/shard_map/all_to_all | solution.py:241
  85.7 0.0 all-gather.3.cloned.1.call-done
  85.8 1.2 %copy-done.1 = f32[256,1024]{1,0:T(8,128)S(1)} copy-done((f32[256,1024]{1,0:T(8,128)S(1)}, f32[256,1024]{1,0:T(8,128)}, u32[]{:S(2)}) %copy-start.1) | copy-done | bytes 1048600
  87.0 0.4 shard_map.126.base_ref
  87.4 8.4 %all-to-all-done.2.back_ref = bf16[64,4,128]{2,1,0:T(4,128)(2,1)S(1)} async-done(((bf16[64,4,128]{2,1,0:T(4,128)(2,1)}), bf16[64,4,128]{2,1,0:T(4,128)(2,1)S(1)}, u32[]{:S(2)}, u32[]{:S(2)}) %all-to-all-start.2) | async-done | bytes 65568 | tf_op jit(solution)/shard_map/all_to_all | solution.py:241
  95.8 1.5 %shard_map.127 = (bf16[16,2,128]{2,1,0:T(2,128)(2,1)}, bf16[16,2,1024]{2,1,0:T(2,128)(2,1)}) custom-call(s32[16]{0:T(128)S(1)} %get-tuple-element.12.place_ref, bf16[64,4,128]{2,1,0:T(4,128)(2,1)S(1)} %all-to-all-done.2.back_ref, f32[32,128]{1,0:T(8,128)S(1)} %shard_map.126.base_ref, f32[256,128]{1,0:T(8,128)S(1)} %get-tuple-element.20.part_ref, ...), custom_call_target="tpu_custom_call" | custom-call | tf_op jit(solution)/shard_map/pallas_call | solution.py:172
  (19 shorter events, 0.0 us)
Async XLA Ops:
  7.2 48.3 %copy-start.3 = (bf16[16,64,128]{2,1,0:T(8,128)(2,1)S(1)}, bf16[16,64,128]{2,1,0:T(8,128)(2,1)}, u32[]{:S(2)}) copy-start(bf16[16,64,128]{2,1,0:T(8,128)(2,1)} %key_ref.1) | copy-start | bytes 786436
  7.2 48.3 %copy-start.4 = (bf16[16,64,128]{2,1,0:T(8,128)(2,1)S(1)}, bf16[16,64,128]{2,1,0:T(8,128)(2,1)}, u32[]{:S(2)}) copy-start(bf16[16,64,128]{2,1,0:T(8,128)(2,1)} %value_ref.2) | copy-start | bytes 786436
  7.2 0.9 copy-start.8
  8.1 0.7 copy-start.11
  8.8 0.7 copy-start.12
  9.4 46.0 %copy-start.9 = (bf16[16,2,1024]{2,1,0:T(2,128)(2,1)S(1)}, bf16[16,2,1024]{2,1,0:T(2,128)(2,1)}, u32[]{:S(2)}) copy-start(bf16[16,2,1024]{2,1,0:T(2,128)(2,1)} %q_ref.1) | copy-start | bytes 196612
  9.4 46.1 %copy-start.10 = (bf16[16,2,128]{2,1,0:T(2,128)(2,1)S(1)}, bf16[16,2,128]{2,1,0:T(2,128)(2,1)}, u32[]{:S(2)}) copy-start(bf16[16,2,128]{2,1,0:T(2,128)(2,1)} %fresh_ref.1) | copy-start | bytes 24580
  9.4 46.1 %copy-start.13 = (s32[16]{0:T(128)S(1)}, s32[16]{0:T(128)}, u32[]{:S(2)}) copy-start(s32[16]{0:T(128)} %length_ref.1) | copy-start | bytes 196
  11.4 63.3 %copy-start.5 = (bf16[512,128]{1,0:T(8,128)(2,1)S(1)}, bf16[512,128]{1,0:T(8,128)(2,1)}, u32[]{:S(2)}) copy-start(bf16[512,128]{1,0:T(8,128)(2,1)} %up_ref.1) | copy-start | bytes 393220
  11.4 34.0 %all-to-all-start = ((bf16[64,4,1152]{2,1,0:T(4,128)(2,1)}), bf16[64,4,1152]{2,1,0:T(4,128)(2,1)S(1)}, u32[]{:S(2)}, u32[]{:S(2)}) async-start(bf16[64,4,1152]{2,1,0:T(4,128)(2,1)} %get-tuple-element.13), calls=%async_computation | async-start | bytes 1179648 | tf_op jit(solution)/shard_map/all_to_all | solution.py:217
  26.3 59.4 %all-gather.3.cloned.1.call-start = ((), (), s32[]{:S(2)}) async-start(), calls=%async_computation.3 | async-start | bytes 1179648 | tf_op jit(solution)/shard_map/all_gather | solution.py:218
  27.1 58.7 %copy-start = (bf16[8192,128]{1,0:T(8,128)(2,1)S(1)}, bf16[8192,128]{1,0:T(8,128)(2,1)}, u32[]{:S(2)}) copy-start(bf16[8192,128]{1,0:T(8,128)(2,1)} %value_ref.3) | copy-start | bytes 6291460
  45.4 1.2 %copy-start.2 = (bf16[1024,512]{1,0:T(8,128)(2,1)S(1)}, bf16[1024,512]{1,0:T(8,128)(2,1)}, u32[]{:S(2)}) copy-start(bf16[1024,512]{1,0:T(8,128)(2,1)} %down_ref.1) | copy-start | bytes 3145732
  47.9 0.7 copy-start.6
  48.6 26.0 %all-to-all-start.1 = ((bf16[8,256,128]{2,1,0:T(8,128)(2,1)}), bf16[8,256,128]{2,1,0:T(8,128)(2,1)S(1)}, u32[]{:S(2)}, u32[]{:S(2)}) async-start(bf16[8,256,128]{2,1,0:T(8,128)(2,1)} %get-tuple-element.14), calls=%async_computation.1 | async-start | bytes 1048576 | tf_op jit(solution)/shard_map/all_to_all | solution.py:233
  74.6 0.9 copy-start.7
  76.5 19.3 %all-to-all-start.2 = ((bf16[64,4,128]{2,1,0:T(4,128)(2,1)}), bf16[64,4,128]{2,1,0:T(4,128)(2,1)S(1)}, u32[]{:S(2)}, u32[]{:S(2)}) async-start(bf16[64,4,128]{2,1,0:T(4,128)(2,1)} %shard_map.125), calls=%async_computation.2 | async-start | bytes 131072 | tf_op jit(solution)/shard_map/all_to_all | solution.py:241
  85.7 1.2 %copy-start.1 = (f32[256,1024]{1,0:T(8,128)S(1)}, f32[256,1024]{1,0:T(8,128)}, u32[]{:S(2)}) copy-start(f32[256,1024]{1,0:T(8,128)} %all-gather.3.cloned.1.call-done) | copy-start | bytes 3145732
Sparse Core Ops, SparseCore 0:
  29.3 42.4 all-gather.2

commit v3 on v2

--- a/solution.py
+++ b/solution.py
@@ -35,10 +35,21 @@
     return jnp.where(iota(shape, 0) == target, 1.0, 0.0).astype(BF)
 
 
-def route_kernel(adapters, adapter_ref, storage_ref, x_ref, send_ref, wide_ref, place_ref):
+def route_kernel(
+    adapters, adapter_hbm, storage_hbm, x_hbm, send_ref, place_ref, adapter_ref, storage_ref, x_ref, sems
+):
+    copies = [
+        pltpu.make_async_copy(adapter_hbm, adapter_ref, sems.at[0]),
+        pltpu.make_async_copy(storage_hbm, storage_ref, sems.at[1]),
+        pltpu.make_async_copy(x_hbm, x_ref, sems.at[2]),
+    ]
+    for copy in copies:
+        copy.start()
     requests, steps, width = x_ref.shape
     homes = send_ref.shape[0]
     rows = homes * CAP * steps
+    copies[0].wait()
+    copies[1].wait()
     storage = [storage_ref[adapter_ref[i]] for i in range(requests)]
     home = [s // adapters for s in storage]
     code = jnp.zeros((requests * steps, LANES), I32)
@@ -49,20 +60,33 @@
             earlier = earlier + (home[k] == home[i]).astype(I32)
         place_ref[i] = home[i] * CAP + earlier
         code = jnp.where(row // steps == i, storage[i] % adapters, code)
+    pick = picker(place_ref, rows, steps, requests)
+    copies[2].wait()
     x = x_ref[...].reshape(requests * steps, width)
-    wide_ref[...] = x.astype(F32)
-    pick = picker(place_ref, rows, steps, requests)
     send = dot(pick, jnp.concatenate([x, code.astype(F32).astype(BF)], axis=1))
     send_ref[...] = send.astype(BF).reshape(send_ref.shape)
 
 
-def down_kernel(halves, seen_ref, down_ref, part_ref, code_ref):
+def down_kernel(halves, seen_ref, down_hbm, part_ref, code_hbm, down_ref, code_ref, sems):
     homes, per, width = seen_ref.shape
     width = width - LANES
+    pieces = down_ref.shape[0]
+    deep = width // pieces
+    copies = [
+        pltpu.make_async_copy(down_hbm.at[pl.ds(k * deep, deep)], down_ref.at[k], sems.at[k])
+        for k in range(pieces)
+    ]
+    for copy in copies:
+        copy.start()
     seen = seen_ref[...].reshape(homes * per, width + LANES)
     code = seen[:, width:].astype(F32)
     code_ref[...] = code
-    product = dot(seen[:, :width], down_ref[...])
+    save = pltpu.make_async_copy(code_ref, code_hbm, sems.at[pieces])
+    save.start()
+    product = jnp.zeros((homes * per, down_ref.shape[2]), F32)
+    for k in range(pieces):
+        copies[k].wait()
+        product = product + dot(seen[:, k * deep : (k + 1) * deep], down_ref[k])
     lane = iota(code.shape, 1)
     own = jnp.zeros(code.shape, F32)
     for m in range(product.shape[1] // LANES):
@@ -79,11 +103,17 @@
     part = jnp.concatenate(pieces, axis=0)
     for t in range(part_ref.shape[0]):
         part_ref[t] = part
-
-
-def up_kernel(halves, part_ref, code_ref, up_ref, back_ref):
-    code = code_ref[...]
-    half = code.shape[0] // 2
+    save.wait()
+
+
+def up_kernel(halves, part_ref, code_hbm, up_hbm, back_ref, code_ref, up_ref, sems):
+    copies = [
+        pltpu.make_async_copy(code_hbm, code_ref, sems.at[0]),
+        pltpu.make_async_copy(up_hbm, up_ref, sems.at[1]),
+    ]
+    for copy in copies:
+        copy.start()
+    half = code_ref.shape[0] // 2
     total = jnp.zeros((half, LANES), F32)
     for t in range(part_ref.shape[0]):
         for k in range(halves):
@@ -94,11 +124,14 @@
     both = jnp.concatenate(
         [jnp.where(left, total, turned), jnp.where(left, turned, total)], axis=0
     )
+    copies[0].wait()
+    code = code_ref[...]
     lane = iota(code.shape, 1)
     spread = []
     for m in range(up_ref.shape[0] // LANES):
         here = (2 * m + lane // ADAPTER_RANK).astype(F32) == code
         spread.append(jnp.where(here, both, 0.0).astype(BF))
+    copies[1].wait()
     back = dot(jnp.concatenate(spread, axis=1), up_ref[...]).astype(BF)
     back_ref[...] = back.reshape(back_ref.shape)
 
@@ -140,11 +173,19 @@
     part_ref[...] = dot((cached / total).astype(BF), values)
 
 
-def base_kernel(wide_ref, value_ref, base_ref):
-    width = wide_ref.shape[2]
+def base_kernel(index_ref, x_ref, far_ref, *refs):
+    value_ref, base_ref = refs[-2:]
+    requests, steps, width = x_ref.shape
+    rows = requests * steps
+    mine = index_ref[0]
+    pieces = [(0, x_ref[...]), (4, far_ref[...])]
+    for k, ref in enumerate(refs[:-2]):
+        pieces.append((k + 1, ref[:requests]))
+        pieces.append((k + 5, ref[requests:]))
     total = jnp.zeros(base_ref.shape, F32)
-    for t in range(wide_ref.shape[0]):
-        total = total + dot(wide_ref[t].astype(BF), value_ref[t * width : (t + 1) * width, :])
+    for other, piece in pieces:
+        start = pl.multiple_of((mine ^ other) * width, width)
+        total = total + dot(piece.reshape(rows, width), value_ref[pl.ds(start, width), :])
     base_ref[...] = total
 
 
@@ -166,15 +207,17 @@
 
 VM = pl.BlockSpec(memory_space=pltpu.VMEM)
 SM = pl.BlockSpec(memory_space=pltpu.SMEM)
-
-
-def call(kernel, ins, outs, args, flops=0, bytes_accessed=0):
+HB = pl.BlockSpec(memory_space=pltpu.HBM)
+
+
+def call(kernel, ins, outs, args, scratch=(), flops=0, bytes_accessed=0, mib=16):
     return pl.pallas_call(
         kernel,
         in_specs=list(ins),
         out_specs=tuple(s for s, _ in outs),
         out_shape=tuple(o for _, o in outs),
-        compiler_params=pltpu.CompilerParams(vmem_limit_bytes=32 * 1024 * 1024),
+        scratch_shapes=list(scratch),
+        compiler_params=pltpu.CompilerParams(vmem_limit_bytes=mib * 1024 * 1024),
         cost_estimate=pl.CostEstimate(
             flops=flops, bytes_accessed=bytes_accessed, transcendentals=0
         ),
@@ -204,18 +247,26 @@
     groups = queries.shape[2] // HEAD_WIDTH
     halves = HALVES
     shape = jax.ShapeDtypeStruct
-    send, wide, place = call(
+    send, place = call(
         functools.partial(route_kernel, A),
-        (SM, SM, VM),
+        (HB, HB, HB),
+        ((VM, shape((H, CAP * S, W + LANES), BF)), (SM, shape((R,), I32))),
+        (request_adapter, adapter_storage_row, x),
         (
-            (VM, shape((H, CAP * S, W + LANES), BF)),
-            (VM, shape((R * S, W), F32)),
-            (SM, shape((R,), I32)),
+            pltpu.SMEM(request_adapter.shape, I32),
+            pltpu.SMEM(adapter_storage_row.shape, I32),
+            pltpu.VMEM(x.shape, BF),
+            pltpu.SemaphoreType.DMA((3,)),
         ),
-        (request_adapter, adapter_storage_row, x),
+        mib=60,
     )
     seen = lax.all_to_all(send, "req", 0, 0)
-    wide = lax.all_gather(wide, "tp", axis=0)
+    x, send = lax.optimization_barrier((x, send))
+    swap = lambda v, d: lax.ppermute(v, "tp", [(i, i ^ d) for i in range(T)])
+    far = swap(x, 4)
+    pair = jnp.concatenate([x, far], axis=0)
+    pairs = [swap(pair, d) for d in (1, 2, 3)]
+    seen, far, pairs = lax.optimization_barrier((seen, far, pairs))
     attended, weights = call(
         scores_kernel,
         (SM, VM, VM, VM, VM),
@@ -223,24 +274,42 @@
         (cache_valid_length, queries, stored_key_cache, stored_value_cache, step_keys),
         flops=10**8,
         bytes_accessed=10**6,
-    )
+        mib=60,
+    )
+    pieces = 4
     part, code = call(
         functools.partial(down_kernel, halves),
-        (VM, VM),
-        ((VM, shape((T, halves * rows // 2, LANES), BF)), (VM, shape((rows, LANES), F32))),
+        (VM, HB),
+        ((VM, shape((T, halves * rows // 2, LANES), BF)), (HB, shape((rows, LANES), F32))),
         (seen, adapter_down_weight),
+        (
+            pltpu.VMEM((pieces, W // pieces, adapter_down_weight.shape[1]), BF),
+            pltpu.VMEM((rows, LANES), F32),
+            pltpu.SemaphoreType.DMA((pieces + 1,)),
+        ),
     )
     part = lax.all_to_all(part, "tp", 0, 0)
     part, attended, weights = lax.optimization_barrier((part, attended, weights))
     (back,) = call(
         functools.partial(up_kernel, halves),
-        (VM, VM, VM),
+        (VM, HB, HB),
         ((VM, shape((H, CAP * S, V), BF)),),
         (part, code, adapter_up_weight),
+        (
+            pltpu.VMEM((rows, LANES), F32),
+            pltpu.VMEM(adapter_up_weight.shape, BF),
+            pltpu.SemaphoreType.DMA((2,)),
+        ),
     )
     back = lax.all_to_all(back, "req", 0, 0)
+    mine = lax.axis_index("tp").astype(I32).reshape(1)
     (base,) = call(
-        base_kernel, (VM, VM), ((VM, shape((R * S, V), F32)),), (wide, value_matrix)
+        base_kernel,
+        (SM, VM, VM) + (VM,) * len(pairs) + (VM,),
+        ((VM, shape((R * S, V), F32)),),
+        (mine, x, far, *pairs, value_matrix),
+        flops=10**8,
+        mib=60,
     )
     step_values, attention = call(
         finish_kernel,

time: 105 us -> 94.2 us (0.90)
  starting transfers between devices: 31.1 us -> 50.7 us
  waiting for transfers between devices: 45.1 us -> 27.9 us
  between operations: 14.2 us -> 0.81 us
  Pallas kernels: 7.57 us -> 12.5 us
  local copies, waits for them, and re-layouts: 6.26 us -> 1.7 us
    all_to_all x1, waiting for transfers between devices: 18.3 us -> 0.01 us  [body(): seen = lax.all_to_all(send, 'req', 0, 0)]
    ppermute x0 -> x4, starting transfers between devices: none -> 17.6 us  [body(): swap = lambda v, d: lax.ppermute(v, 'tp', [(i, i ^ d) for i in range(T)])]
    ppermute x0 -> x4, waiting for transfers between devices: none -> 8.56 us  [body(): swap = lambda v, d: lax.ppermute(v, 'tp', [(i, i ^ d) for i in range(T)])]
    all_to_all x1, waiting for transfers between devices: 17.7 us -> 12.2 us  [body(): part = lax.all_to_all(part, 'tp', 0, 0)]
    pallas_call x6, Pallas kernels: 7.57 us -> 12.5 us  [call(): pl.pallas_call(kernel, in_specs=list(ins), out_specs=tuple((s for s, _ in...]
    unnamed x28 -> x21, local copies, waits for them, and re-layouts: 6.26 us -> 1.64 us
    all_to_all x1, starting transfers between devices: 9.23 us -> 13.4 us  [body(): back = lax.all_to_all(back, 'req', 0, 0)]
    all_to_all x1, starting transfers between devices: 6.84 us -> 4.77 us  [body(): part = lax.all_to_all(part, 'tp', 0, 0)]
  transfers between devices with their start and end apart: 4 -> 7, of which waited for: 3 -> 4; matrix products, arithmetic and copies ran while one was open for 0% -> 1% of each run, Pallas kernels for 4% -> 6%
where the time goes in v3:
time: 94.2 us; the launch traced here: 93.6 us
  starting transfers between devices  50.7 us (54%)
  waiting for transfers between devices  27.9 us (30%)
  Pallas kernels  12.5 us (13%)
  local copies, waits for them, and re-layouts  1.7 us (2%)
    ppermute x4, starting transfers between devices, body(): swap = lambda v, d: lax.ppermute(v, 'tp', [(i, i ^ d) for i in range(T)])  17.6 us
    all_to_all x1, starting transfers between devices, body(): seen = lax.all_to_all(send, 'req', 0, 0)  15 us
    all_to_all x1, starting transfers between devices, body(): back = lax.all_to_all(back, 'req', 0, 0)  13.4 us
    pallas_call x6, Pallas kernels, call(): pl.pallas_call(kernel, in_specs=list(ins), out_specs=tuple((s for s, _ in...  12.5 us
    all_to_all x1, waiting for transfers between devices, body(): part = lax.all_to_all(part, 'tp', 0, 0)  12.2 us
    ppermute x4, waiting for transfers between devices, body(): swap = lambda v, d: lax.ppermute(v, 'tp', [(i, i ^ d) for i in range(T)])  8.56 us
    all_to_all x1, waiting for transfers between devices, body(): back = lax.all_to_all(back, 'req', 0, 0)  7.16 us
    all_to_all x1, starting transfers between devices, body(): part = lax.all_to_all(part, 'tp', 0, 0)  4.77 us
  transfers between devices with their start and end apart: 7, of which 4 were waited for; matrix products, arithmetic and copies ran while one was open for 1% of the time, Pallas kernels for 6%

profile of v3, /device:TPU:1, one launch (start us, length us, event | category | flops | bytes accessed | tf_op | source)
XLA Modules:
  0.0 93.6 jit_solution(9229919232107350709)
XLA Ops:
  0.6 2.3 %shard_map.122 = (bf16[64,4,1152]{2,1,0:T(4,128)(2,1)}, s32[16]{0:T(128)}) custom-call(s32[16]{0:T(128)} %adapter_hbm.1, s32[512]{0:T(512)} %storage_hbm.1, bf16[16,2,1024]{2,1,0:T(2,128)(2,1)} %x_ref), custom_call_target="tpu_custom_call" | custom-call | tf_op jit(solution)/shard_map/pallas_call | solution.py:214
  2.9 0.0 copy-start.2
  2.9 15.0 %all-to-all-start = ((bf16[64,4,1152]{2,1,0:T(4,128)(2,1)}), bf16[64,4,1152]{2,1,0:T(4,128)(2,1)S(1)}, u32[]{:S(2)}, u32[]{:S(2)}) async-start(bf16[64,4,1152]{2,1,0:T(4,128)(2,1)} %get-tuple-element.18), calls=%async_computation | async-start | bytes 1179648 | tf_op jit(solution)/shard_map/all_to_all | solution.py:263
  17.9 7.5 %collective-permute-start = (bf16[16,2,1024]{2,1,0:T(2,128)(2,1)}, bf16[16,2,1024]{2,1,0:T(2,128)(2,1)S(1)}, u32[]{:S(2)}, u32[]{:S(2)}) collective-permute-start(bf16[16,2,1024]{2,1,0:T(2,128)(2,1)} %x_ref), channel_id=1, source_target_pairs={{0,4},{1,5},{2,6},{3,7},{4,0},{5,1},{6,2},{7,3},{8,12},{9,13},{10,... | collective-permute-start | bytes 196616 | tf_op jit(solution)/shard_map/ppermute | solution.py:265
  25.4 0.9 constant_dynamic-update-slice_fusion.1
  26.3 1.2 %collective-permute-done.far_ref = bf16[16,2,1024]{2,1,0:T(2,128)(2,1)S(1)} collective-permute-done((bf16[16,2,1024]{2,1,0:T(2,128)(2,1)}, bf16[16,2,1024]{2,1,0:T(2,128)(2,1)S(1)}, u32[]{:S(2)}, u32[]{:S(2)}) %collective-permute-start) | collective-permute-done | bytes 65568 | tf_op jit(solution)/shard_map/ppermute | solution.py:265
  27.5 0.1 constant_dynamic-update-slice_fusion
  27.6 5.1 %collective-permute-start.3 = (bf16[32,2,1024]{2,1,0:T(2,128)(2,1)S(1)}, bf16[32,2,1024]{2,1,0:T(2,128)(2,1)S(1)}, u32[]{:S(2)}, u32[]{:S(2)}) collective-permute-start(bf16[32,2,1024]{2,1,0:T(2,128)(2,1)S(1)} %constant_dynamic-update-slice_fusion), channel_id=1, source_target_pairs={{0,3},{1,2},{2,1},{3,0},{4,7},{5,6},{6,5},{7,4},{8,11},{9,10},{10,... | collective-permute-start | bytes 393224 | tf_op jit(solution)/shard_map/ppermute | solution.py:265
  32.6 2.9 %collective-permute-start.2 = (bf16[32,2,1024]{2,1,0:T(2,128)(2,1)S(1)}, bf16[32,2,1024]{2,1,0:T(2,128)(2,1)S(1)}, u32[]{:S(2)}, u32[]{:S(2)}) collective-permute-start(bf16[32,2,1024]{2,1,0:T(2,128)(2,1)S(1)} %constant_dynamic-update-slice_fusion), channel_id=1, source_target_pairs={{0,2},{1,3},{2,0},{3,1},{4,6},{5,7},{6,4},{7,5},{8,10},{9,11},{10,... | collective-permute-start | bytes 393224 | tf_op jit(solution)/shard_map/ppermute | solution.py:265
  35.5 2.2 %collective-permute-start.1 = (bf16[32,2,1024]{2,1,0:T(2,128)(2,1)S(1)}, bf16[32,2,1024]{2,1,0:T(2,128)(2,1)S(1)}, u32[]{:S(2)}, u32[]{:S(2)}) collective-permute-start(bf16[32,2,1024]{2,1,0:T(2,128)(2,1)S(1)} %constant_dynamic-update-slice_fusion), channel_id=1, source_target_pairs={{0,1},{1,0},{2,3},{3,2},{4,5},{5,4},{6,7},{7,6},{8,9},{9,8},{10,11... | collective-permute-start | bytes 393224 | tf_op jit(solution)/shard_map/ppermute | solution.py:265
  37.7 0.0 collective-permute-done.3.refs_2_
  37.7 7.3 %collective-permute-done.2.refs_1_ = bf16[32,2,1024]{2,1,0:T(2,128)(2,1)S(1)} collective-permute-done((bf16[32,2,1024]{2,1,0:T(2,128)(2,1)S(1)}, bf16[32,2,1024]{2,1,0:T(2,128)(2,1)S(1)}, u32[]{:S(2)}, u32[]{:S(2)}) %collective-permute-start.2) | collective-permute-done | bytes 131104 | tf_op jit(solution)/shard_map/ppermute | solution.py:265
  45.0 0.0 collective-permute-done.1.refs_0_
  45.0 0.0 all-to-all-done.seen_ref
  45.1 1.8 %shard_map.123 = (bf16[8,256,128]{2,1,0:T(8,128)(2,1)}, f32[256,128]{1,0:T(8,128)S(1)}) custom-call(bf16[64,4,1152]{2,1,0:T(4,128)(2,1)S(1)} %all-to-all-done.seen_ref, bf16[1024,512]{1,0:T(8,128)(2,1)S(1)} %copy-done), custom_call_target="tpu_custom_call" | custom-call | tf_op jit(solution)/shard_map/pallas_call | solution.py:214
  46.9 4.8 %all-to-all-start.1 = ((bf16[8,256,128]{2,1,0:T(8,128)(2,1)}), bf16[8,256,128]{2,1,0:T(8,128)(2,1)S(1)}, u32[]{:S(2)}, u32[]{:S(2)}) async-start(bf16[8,256,128]{2,1,0:T(8,128)(2,1)} %get-tuple-element.21), calls=%async_computation.1 | async-start | bytes 1048576 | tf_op jit(solution)/shard_map/all_to_all | solution.py:291
  51.6 2.6 %shard_map.124 = (f32[256,128]{1,0:T(8,128)}, bf16[256,32]{1,0:T(8,128)(2,1)}) custom-call(s32[16]{0:T(128)} %length_ref.1, bf16[16,2,1024]{2,1,0:T(2,128)(2,1)} %q_ref.1, bf16[16,64,128]{2,1,0:T(8,128)(2,1)} %key_ref.1, bf16[16,64,128]{2,1,0:T(8,128)(2,1)} %value_ref.1, bf16[16,2,128]{2,1,0:T(2,128)(2,1)} %fresh_ref.1), custom_call_target="tpu_custom_call" | custom-call | flops 100000000 | bytes 1000000 | tf_op jit(solution)/shard_map/pallas_call | solution.py:214
  54.3 12.2 %all-to-all-done.1.part_ref = bf16[8,256,128]{2,1,0:T(8,128)(2,1)S(1)} async-done(((bf16[8,256,128]{2,1,0:T(8,128)(2,1)}), bf16[8,256,128]{2,1,0:T(8,128)(2,1)S(1)}, u32[]{:S(2)}, u32[]{:S(2)}) %all-to-all-start.1) | async-done | bytes 524320 | tf_op jit(solution)/shard_map/all_to_all | solution.py:291
  66.5 1.4 %shard_map.125 = bf16[64,4,128]{2,1,0:T(4,128)(2,1)} custom-call(bf16[8,256,128]{2,1,0:T(8,128)(2,1)S(1)} %all-to-all-done.1.part_ref, f32[256,128]{1,0:T(8,128)S(1)} %get-tuple-element.25.code_hbm, bf16[512,128]{1,0:T(8,128)(2,1)S(1)} %copy-done.2), custom_call_target="tpu_custom_call" | custom-call | tf_op jit(solution)/shard_map/pallas_call | solution.py:214
  67.9 13.4 %all-to-all-start.2 = ((bf16[64,4,128]{2,1,0:T(4,128)(2,1)}), bf16[64,4,128]{2,1,0:T(4,128)(2,1)S(1)}, u32[]{:S(2)}, u32[]{:S(2)}) async-start(bf16[64,4,128]{2,1,0:T(4,128)(2,1)} %shard_map.125), calls=%async_computation.2 | async-start | bytes 131072 | tf_op jit(solution)/shard_map/all_to_all | solution.py:304
  81.3 2.9 %shard_map.126.base_ref = f32[32,128]{1,0:T(8,128)} custom-call(s32[1]{0:T(128)} %bitcast.index_ref, bf16[16,2,1024]{2,1,0:T(2,128)(2,1)} %x_ref, bf16[16,2,1024]{2,1,0:T(2,128)(2,1)} %copy-done.6, bf16[32,2,1024]{2,1,0:T(2,128)(2,1)} %copy-done.9, bf16[32,2,1024]{2,1,0:T(2,128)(2,1)} %copy-done.8, bf16[32,2,1024]{2,1,0:T(2,128)(2,1)} %copy-done.7, ...), custom_call_target="tpu_custom_call" | custom-call | flops 100000000 | tf_op jit(solution)/shard_map/pallas_call | solution.py:214
  84.2 7.2 %all-to-all-done.2.back_ref = bf16[64,4,128]{2,1,0:T(4,128)(2,1)S(1)} async-done(((bf16[64,4,128]{2,1,0:T(4,128)(2,1)}), bf16[64,4,128]{2,1,0:T(4,128)(2,1)S(1)}, u32[]{:S(2)}, u32[]{:S(2)}) %all-to-all-start.2) | async-done | bytes 65568 | tf_op jit(solution)/shard_map/all_to_all | solution.py:304
  91.4 0.7 copy-done.3
  92.1 1.5 %shard_map.127 = (bf16[16,2,128]{2,1,0:T(2,128)(2,1)}, bf16[16,2,1024]{2,1,0:T(2,128)(2,1)}) custom-call(s32[16]{0:T(128)S(1)} %copy-done.5, bf16[64,4,128]{2,1,0:T(4,128)(2,1)S(1)} %all-to-all-done.2.back_ref, f32[32,128]{1,0:T(8,128)S(1)} %copy-done.3, f32[256,128]{1,0:T(8,128)S(1)} %copy-done.1, bf16[256,32]{1,0:T(8,128)(2,1)S(1)} %copy-done.4), custom_call_target="tpu_custom_call" | custom-call | tf_op jit(solution)/shard_map/pallas_call | solution.py:214
  (18 shorter events, 0.0 us)
Async XLA Ops:
  0.6 44.4 %copy-start = (bf16[1024,512]{1,0:T(8,128)(2,1)S(1)}, bf16[1024,512]{1,0:T(8,128)(2,1)}, u32[]{:S(2)}) copy-start(bf16[1024,512]{1,0:T(8,128)(2,1)} %down_hbm.1) | copy-start | bytes 3145732
  2.9 63.6 %copy-start.2 = (bf16[512,128]{1,0:T(8,128)(2,1)S(1)}, bf16[512,128]{1,0:T(8,128)(2,1)}, u32[]{:S(2)}) copy-start(bf16[512,128]{1,0:T(8,128)(2,1)} %up_hbm.1) | copy-start | bytes 393220
  2.9 42.1 %all-to-all-start = ((bf16[64,4,1152]{2,1,0:T(4,128)(2,1)}), bf16[64,4,1152]{2,1,0:T(4,128)(2,1)S(1)}, u32[]{:S(2)}, u32[]{:S(2)}) async-start(bf16[64,4,1152]{2,1,0:T(4,128)(2,1)} %get-tuple-element.18), calls=%async_computation | async-start | bytes 1179648 | tf_op jit(solution)/shard_map/all_to_all | solution.py:263
  17.9 9.6 %collective-permute-start = (bf16[16,2,1024]{2,1,0:T(2,128)(2,1)}, bf16[16,2,1024]{2,1,0:T(2,128)(2,1)S(1)}, u32[]{:S(2)}, u32[]{:S(2)}) collective-permute-start(bf16[16,2,1024]{2,1,0:T(2,128)(2,1)} %x_ref), channel_id=1, source_target_pairs={{0,4},{1,5},{2,6},{3,7},{4,0},{5,1},{6,2},{7,3},{8,12},{9,13},{10,... | collective-permute-start | bytes 196616 | tf_op jit(solution)/shard_map/ppermute | solution.py:265
  27.5 40.4 %copy-start.6 = (bf16[16,2,1024]{2,1,0:T(2,128)(2,1)}, bf16[16,2,1024]{2,1,0:T(2,128)(2,1)S(1)}, u32[]{:S(2)}) copy-start(bf16[16,2,1024]{2,1,0:T(2,128)(2,1)S(1)} %collective-permute-done.far_ref) | copy-start | bytes 196612
  27.6 10.1 %collective-permute-start.3 = (bf16[32,2,1024]{2,1,0:T(2,128)(2,1)S(1)}, bf16[32,2,1024]{2,1,0:T(2,128)(2,1)S(1)}, u32[]{:S(2)}, u32[]{:S(2)}) collective-permute-start(bf16[32,2,1024]{2,1,0:T(2,128)(2,1)S(1)} %constant_dynamic-update-slice_fusion), channel_id=1, source_target_pairs={{0,3},{1,2},{2,1},{3,0},{4,7},{5,6},{6,5},{7,4},{8,11},{9,10},{10,... | collective-permute-start | bytes 393224 | tf_op jit(solution)/shard_map/ppermute | solution.py:265
  32.6 12.4 %collective-permute-start.2 = (bf16[32,2,1024]{2,1,0:T(2,128)(2,1)S(1)}, bf16[32,2,1024]{2,1,0:T(2,128)(2,1)S(1)}, u32[]{:S(2)}, u32[]{:S(2)}) collective-permute-start(bf16[32,2,1024]{2,1,0:T(2,128)(2,1)S(1)} %constant_dynamic-update-slice_fusion), channel_id=1, source_target_pairs={{0,2},{1,3},{2,0},{3,1},{4,6},{5,7},{6,4},{7,5},{8,10},{9,11},{10,... | collective-permute-start | bytes 393224 | tf_op jit(solution)/shard_map/ppermute | solution.py:265
  35.5 9.5 %collective-permute-start.1 = (bf16[32,2,1024]{2,1,0:T(2,128)(2,1)S(1)}, bf16[32,2,1024]{2,1,0:T(2,128)(2,1)S(1)}, u32[]{:S(2)}, u32[]{:S(2)}) collective-permute-start(bf16[32,2,1024]{2,1,0:T(2,128)(2,1)S(1)} %constant_dynamic-update-slice_fusion), channel_id=1, source_target_pairs={{0,1},{1,0},{2,3},{3,2},{4,5},{5,4},{6,7},{7,6},{8,9},{9,8},{10,11... | collective-permute-start | bytes 393224 | tf_op jit(solution)/shard_map/ppermute | solution.py:265
  37.7 30.2 %copy-start.7 = (bf16[32,2,1024]{2,1,0:T(2,128)(2,1)}, bf16[32,2,1024]{2,1,0:T(2,128)(2,1)S(1)}, u32[]{:S(2)}) copy-start(bf16[32,2,1024]{2,1,0:T(2,128)(2,1)S(1)} %collective-permute-done.3.refs_2_) | copy-start | bytes 393220
  45.0 22.8 %copy-start.8 = (bf16[32,2,1024]{2,1,0:T(2,128)(2,1)}, bf16[32,2,1024]{2,1,0:T(2,128)(2,1)S(1)}, u32[]{:S(2)}) copy-start(bf16[32,2,1024]{2,1,0:T(2,128)(2,1)S(1)} %collective-permute-done.2.refs_1_) | copy-start | bytes 393220
  45.0 22.9 %copy-start.9 = (bf16[32,2,1024]{2,1,0:T(2,128)(2,1)}, bf16[32,2,1024]{2,1,0:T(2,128)(2,1)S(1)}, u32[]{:S(2)}) copy-start(bf16[32,2,1024]{2,1,0:T(2,128)(2,1)S(1)} %collective-permute-done.1.refs_0_) | copy-start | bytes 393220
  46.9 19.6 %all-to-all-start.1 = ((bf16[8,256,128]{2,1,0:T(8,128)(2,1)}), bf16[8,256,128]{2,1,0:T(8,128)(2,1)S(1)}, u32[]{:S(2)}, u32[]{:S(2)}) async-start(bf16[8,256,128]{2,1,0:T(8,128)(2,1)} %get-tuple-element.21), calls=%async_computation.1 | async-start | bytes 1048576 | tf_op jit(solution)/shard_map/all_to_all | solution.py:291
  51.6 39.7 %copy-start.5 = (s32[16]{0:T(128)S(1)}, s32[16]{0:T(128)}, u32[]{:S(2)}) copy-start(s32[16]{0:T(128)} %get-tuple-element.17.place_ref) | copy-start | bytes 196
  54.3 37.1 %copy-start.1 = (f32[256,128]{1,0:T(8,128)S(1)}, f32[256,128]{1,0:T(8,128)}, u32[]{:S(2)}) copy-start(f32[256,128]{1,0:T(8,128)} %get-tuple-element.30.part_ref) | copy-start | bytes 393220
  54.3 37.1 %copy-start.4 = (bf16[256,32]{1,0:T(8,128)(2,1)S(1)}, bf16[256,32]{1,0:T(8,128)(2,1)}, u32[]{:S(2)}) copy-start(bf16[256,32]{1,0:T(8,128)(2,1)} %get-tuple-element.31.weight_ref) | copy-start | bytes 49156
  67.9 23.5 %all-to-all-start.2 = ((bf16[64,4,128]{2,1,0:T(4,128)(2,1)}), bf16[64,4,128]{2,1,0:T(4,128)(2,1)S(1)}, u32[]{:S(2)}, u32[]{:S(2)}) async-start(bf16[64,4,128]{2,1,0:T(4,128)(2,1)} %shard_map.125), calls=%async_computation.2 | async-start | bytes 131072 | tf_op jit(solution)/shard_map/all_to_all | solution.py:304
  91.4 0.7 copy-start.3

commit v4 on v3

--- a/solution.py
+++ b/solution.py
@@ -265,8 +265,7 @@
     swap = lambda v, d: lax.ppermute(v, "tp", [(i, i ^ d) for i in range(T)])
     far = swap(x, 4)
     pair = jnp.concatenate([x, far], axis=0)
-    pairs = [swap(pair, d) for d in (1, 2, 3)]
-    seen, far, pairs = lax.optimization_barrier((seen, far, pairs))
+    pairs = [swap(pair, d) for d in (3,)]
     attended, weights = call(
         scores_kernel,
         (SM, VM, VM, VM, VM),
@@ -275,6 +274,9 @@
         flops=10**8,
         bytes_accessed=10**6,
         mib=60,
+    )
+    seen, far, pair, pairs, attended, weights = lax.optimization_barrier(
+        (seen, far, pair, pairs, attended, weights)
     )
     pieces = 4
     part, code = call(
@@ -288,8 +290,11 @@
             pltpu.SemaphoreType.DMA((pieces + 1,)),
         ),
     )
+    part, pair = lax.optimization_barrier((part, pair))
+    near = [swap(pair, d) for d in (1, 2)]
     part = lax.all_to_all(part, "tp", 0, 0)
-    part, attended, weights = lax.optimization_barrier((part, attended, weights))
+    part, near = lax.optimization_barrier((part, near))
+    pairs = near + pairs
     (back,) = call(
         functools.partial(up_kernel, halves),
         (VM, HB, HB),
@@ -309,7 +314,7 @@
         ((VM, shape((R * S, V), F32)),),
         (mine, x, far, *pairs, value_matrix),
         flops=10**8,
-        mib=60,
+        mib=52,
     )
     step_values, attention = call(
         finish_kernel,
@@ -320,7 +325,7 @@
     return (step_values, attention)
 
 
-HALVES = 2
+HALVES = 1
 
 
 def solution(mesh):

time: 94.2 us -> 85.3 us (0.906)
  waiting for transfers between devices: 27.9 us -> 16.9 us
  starting transfers between devices: 50.7 us -> 54.5 us
  Pallas kernels: 12.5 us -> 11.5 us
    all_to_all x1, waiting for transfers between devices: 12.2 us -> 0.01 us  [body(): part = lax.all_to_all(part, 'tp', 0, 0)]
    ppermute x4, starting transfers between devices: 17.6 us -> 20 us  [body(): swap = lambda v, d: lax.ppermute(v, 'tp', [(i, i ^ d) for i in range(T)])]
    all_to_all x1, starting transfers between devices: 4.77 us -> 6.97 us  [body(): part = lax.all_to_all(part, 'tp', 0, 0)]
    all_to_all x1, waiting for transfers between devices: 0.01 us -> 1.43 us  [body(): seen = lax.all_to_all(send, 'req', 0, 0)]
    ppermute x4, waiting for transfers between devices: 8.56 us -> 7.49 us  [body(): swap = lambda v, d: lax.ppermute(v, 'tp', [(i, i ^ d) for i in range(T)])]
    pallas_call x6, Pallas kernels: 12.5 us -> 11.5 us  [call(): pl.pallas_call(kernel, in_specs=list(ins), out_specs=tuple((s for s, _ in...]
  transfers between devices with their start and end apart: 7 -> 7, of which waited for: 4 -> 6; matrix products, arithmetic and copies ran while one was open for 1% -> 1% of each run, Pallas kernels for 6% -> 6%
where the time goes in v4:
time: 85.3 us; the launch traced here: 84.7 us
  starting transfers between devices  54.5 us (64%)
  waiting for transfers between devices  16.9 us (20%)
  Pallas kernels  11.5 us (13%)
  local copies, waits for them, and re-layouts  0.98 us (1%)
    ppermute x4, starting transfers between devices, body(): swap = lambda v, d: lax.ppermute(v, 'tp', [(i, i ^ d) for i in range(T)])  20 us
    all_to_all x1, starting transfers between devices, body(): seen = lax.all_to_all(send, 'req', 0, 0)  15 us
    all_to_all x1, starting transfers between devices, body(): back = lax.all_to_all(back, 'req', 0, 0)  12.6 us
    pallas_call x6, Pallas kernels, call(): pl.pallas_call(kernel, in_specs=list(ins), out_specs=tuple((s for s, _ in...  11.5 us
    all_to_all x1, waiting for transfers between devices, body(): back = lax.all_to_all(back, 'req', 0, 0)  8.03 us
    ppermute x4, waiting for transfers between devices, body(): swap = lambda v, d: lax.ppermute(v, 'tp', [(i, i ^ d) for i in range(T)])  7.49 us
    all_to_all x1, starting transfers between devices, body(): part = lax.all_to_all(part, 'tp', 0, 0)  6.97 us
  transfers between devices with their start and end apart: 7, of which 6 were waited for; matrix products, arithmetic and copies ran while one was open for 1% of the time, Pallas kernels for 6%

profile of v4, /device:TPU:1, one launch (start us, length us, event | category | flops | bytes accessed | tf_op | source)
XLA Modules:
  0.0 84.7 jit_solution(8741590680811794041)
XLA Ops:
  0.6 2.3 %shard_map.122 = (bf16[64,4,1152]{2,1,0:T(4,128)(2,1)}, s32[16]{0:T(128)}) custom-call(s32[16]{0:T(128)} %adapter_hbm.1, s32[512]{0:T(512)} %storage_hbm.1, bf16[16,2,1024]{2,1,0:T(2,128)(2,1)} %x_ref), custom_call_target="tpu_custom_call" | custom-call | tf_op jit(solution)/shard_map/pallas_call | solution.py:214
  2.9 0.0 copy-start.3
  2.9 15.0 %all-to-all-start = ((bf16[64,4,1152]{2,1,0:T(4,128)(2,1)}), bf16[64,4,1152]{2,1,0:T(4,128)(2,1)S(1)}, u32[]{:S(2)}, u32[]{:S(2)}) async-start(bf16[64,4,1152]{2,1,0:T(4,128)(2,1)} %get-tuple-element.21), calls=%async_computation | async-start | bytes 1179648 | tf_op jit(solution)/shard_map/all_to_all | solution.py:263
  17.9 0.0 copy-start.1
  17.9 7.6 %collective-permute-start = (bf16[16,2,1024]{2,1,0:T(2,128)(2,1)}, bf16[16,2,1024]{2,1,0:T(2,128)(2,1)S(1)}, u32[]{:S(2)}, u32[]{:S(2)}) collective-permute-start(bf16[16,2,1024]{2,1,0:T(2,128)(2,1)} %x_ref), channel_id=1, source_target_pairs={{0,4},{1,5},{2,6},{3,7},{4,0},{5,1},{6,2},{7,3},{8,12},{9,13},{10,... | collective-permute-start | bytes 196616 | tf_op jit(solution)/shard_map/ppermute | solution.py:265
  25.5 0.9 %constant_dynamic-update-slice_fusion.1 = bf16[32,2,1024]{2,1,0:T(2,128)(2,1)S(1)} fusion(bf16[16,2,1024]{2,1,0:T(2,128)(2,1)} %x_ref), kind=kLoop, calls=%fused_computation.1 | loop fusion | bytes 131072
  26.4 1.2 %collective-permute-done.far_ref = bf16[16,2,1024]{2,1,0:T(2,128)(2,1)S(1)} collective-permute-done((bf16[16,2,1024]{2,1,0:T(2,128)(2,1)}, bf16[16,2,1024]{2,1,0:T(2,128)(2,1)S(1)}, u32[]{:S(2)}, u32[]{:S(2)}) %collective-permute-start) | collective-permute-done | bytes 65568 | tf_op jit(solution)/shard_map/ppermute | solution.py:265
  27.7 0.1 constant_dynamic-update-slice_fusion
  27.7 5.1 %collective-permute-start.1 = (bf16[32,2,1024]{2,1,0:T(2,128)(2,1)S(1)}, bf16[32,2,1024]{2,1,0:T(2,128)(2,1)S(1)}, u32[]{:S(2)}, u32[]{:S(2)}) collective-permute-start(bf16[32,2,1024]{2,1,0:T(2,128)(2,1)S(1)} %constant_dynamic-update-slice_fusion), channel_id=1, source_target_pairs={{0,3},{1,2},{2,1},{3,0},{4,7},{5,6},{6,5},{7,4},{8,11},{9,10},{10,... | collective-permute-start | bytes 393224 | tf_op jit(solution)/shard_map/ppermute | solution.py:265
  32.8 2.6 %shard_map.123 = (f32[256,128]{1,0:T(8,128)}, bf16[256,32]{1,0:T(8,128)(2,1)}) custom-call(s32[16]{0:T(128)} %length_ref.1, bf16[16,2,1024]{2,1,0:T(2,128)(2,1)} %q_ref.1, bf16[16,64,128]{2,1,0:T(8,128)(2,1)} %key_ref.1, bf16[16,64,128]{2,1,0:T(8,128)(2,1)} %value_ref.1, bf16[16,2,128]{2,1,0:T(2,128)(2,1)} %fresh_ref.1), custom_call_target="tpu_custom_call" | custom-call | flops 100000000 | bytes 1000000 | tf_op jit(solution)/shard_map/pallas_call | solution.py:214
  35.4 0.1 collective-permute-done.1.refs_2_
  35.5 1.4 %all-to-all-done.seen_ref = bf16[64,4,1152]{2,1,0:T(4,128)(2,1)S(1)} async-done(((bf16[64,4,1152]{2,1,0:T(4,128)(2,1)}), bf16[64,4,1152]{2,1,0:T(4,128)(2,1)S(1)}, u32[]{:S(2)}, u32[]{:S(2)}) %all-to-all-start) | async-done | bytes 589856 | tf_op jit(solution)/shard_map/all_to_all | solution.py:263
  36.9 1.7 %shard_map.124 = (bf16[8,128,128]{2,1,0:T(8,128)(2,1)}, f32[256,128]{1,0:T(8,128)S(1)}) custom-call(bf16[64,4,1152]{2,1,0:T(4,128)(2,1)S(1)} %all-to-all-done.seen_ref, bf16[1024,512]{1,0:T(8,128)(2,1)S(1)} %copy-done), custom_call_target="tpu_custom_call" | custom-call | tf_op jit(solution)/shard_map/pallas_call | solution.py:214
  38.6 0.0 copy-start.5
  38.7 7.0 %all-to-all-start.1 = ((bf16[8,128,128]{2,1,0:T(8,128)(2,1)}), bf16[8,128,128]{2,1,0:T(8,128)(2,1)S(1)}, u32[]{:S(2)}, u32[]{:S(2)}) async-start(bf16[8,128,128]{2,1,0:T(8,128)(2,1)} %get-tuple-element.28), calls=%async_computation.1 | async-start | bytes 524288 | tf_op jit(solution)/shard_map/all_to_all | solution.py:295
  45.6 3.4 %collective-permute-start.2 = (bf16[32,2,1024]{2,1,0:T(2,128)(2,1)S(1)}, bf16[32,2,1024]{2,1,0:T(2,128)(2,1)S(1)}, u32[]{:S(2)}, u32[]{:S(2)}) collective-permute-start(bf16[32,2,1024]{2,1,0:T(2,128)(2,1)S(1)} %constant_dynamic-update-slice_fusion), channel_id=1, source_target_pairs={{0,1},{1,0},{2,3},{3,2},{4,5},{5,4},{6,7},{7,6},{8,9},{9,8},{10,11... | collective-permute-start | bytes 393224 | tf_op jit(solution)/shard_map/ppermute | solution.py:265
  49.0 4.0 %collective-permute-start.3 = (bf16[32,2,1024]{2,1,0:T(2,128)(2,1)S(1)}, bf16[32,2,1024]{2,1,0:T(2,128)(2,1)S(1)}, u32[]{:S(2)}, u32[]{:S(2)}) collective-permute-start(bf16[32,2,1024]{2,1,0:T(2,128)(2,1)S(1)} %constant_dynamic-update-slice_fusion), channel_id=1, source_target_pairs={{0,2},{1,3},{2,0},{3,1},{4,6},{5,7},{6,4},{7,5},{8,10},{9,11},{10,... | collective-permute-start | bytes 393224 | tf_op jit(solution)/shard_map/ppermute | solution.py:265
  53.0 1.3 %collective-permute-done.2.refs_0_ = bf16[32,2,1024]{2,1,0:T(2,128)(2,1)S(1)} collective-permute-done((bf16[32,2,1024]{2,1,0:T(2,128)(2,1)S(1)}, bf16[32,2,1024]{2,1,0:T(2,128)(2,1)S(1)}, u32[]{:S(2)}, u32[]{:S(2)}) %collective-permute-start.2) | collective-permute-done | bytes 131104 | tf_op jit(solution)/shard_map/ppermute | solution.py:265
  54.3 4.8 %collective-permute-done.3.refs_1_ = bf16[32,2,1024]{2,1,0:T(2,128)(2,1)S(1)} collective-permute-done((bf16[32,2,1024]{2,1,0:T(2,128)(2,1)S(1)}, bf16[32,2,1024]{2,1,0:T(2,128)(2,1)S(1)}, u32[]{:S(2)}, u32[]{:S(2)}) %collective-permute-start.3) | collective-permute-done | bytes 131104 | tf_op jit(solution)/shard_map/ppermute | solution.py:265
  59.1 1.4 %shard_map.125 = bf16[64,4,128]{2,1,0:T(4,128)(2,1)} custom-call(bf16[8,128,128]{2,1,0:T(8,128)(2,1)S(1)} %all-to-all-done.1.part_ref, f32[256,128]{1,0:T(8,128)S(1)} %get-tuple-element.31.code_hbm, bf16[512,128]{1,0:T(8,128)(2,1)S(1)} %copy-done.3), custom_call_target="tpu_custom_call" | custom-call | tf_op jit(solution)/shard_map/pallas_call | solution.py:214
  60.5 12.6 %all-to-all-start.2 = ((bf16[64,4,128]{2,1,0:T(4,128)(2,1)}), bf16[64,4,128]{2,1,0:T(4,128)(2,1)S(1)}, u32[]{:S(2)}, u32[]{:S(2)}) async-start(bf16[64,4,128]{2,1,0:T(4,128)(2,1)} %shard_map.125), calls=%async_computation.2 | async-start | bytes 131072 | tf_op jit(solution)/shard_map/all_to_all | solution.py:309
  73.1 2.0 %shard_map.126.base_ref = f32[32,128]{1,0:T(8,128)S(1)} custom-call(s32[1]{0:T(128)} %bitcast.index_ref, bf16[16,2,1024]{2,1,0:T(2,128)(2,1)S(1)} %copy-done.1, bf16[16,2,1024]{2,1,0:T(2,128)(2,1)S(1)} %collective-permute-done.far_ref, bf16[32,2,1024]{2,1,0:T(2,128)(2,1)S(1)} %collective-permute-done.2.refs_0_, ...), custom_call_target="tpu_custom_call" | custom-call | flops 100000000 | tf_op jit(solution)/shard_map/pallas_call | solution.py:214
  75.1 8.0 %all-to-all-done.2.back_ref = bf16[64,4,128]{2,1,0:T(4,128)(2,1)S(1)} async-done(((bf16[64,4,128]{2,1,0:T(4,128)(2,1)}), bf16[64,4,128]{2,1,0:T(4,128)(2,1)S(1)}, u32[]{:S(2)}, u32[]{:S(2)}) %all-to-all-start.2) | async-done | bytes 65568 | tf_op jit(solution)/shard_map/all_to_all | solution.py:309
  83.2 1.5 %shard_map.127 = (bf16[16,2,128]{2,1,0:T(2,128)(2,1)}, bf16[16,2,1024]{2,1,0:T(2,128)(2,1)}) custom-call(s32[16]{0:T(128)S(1)} %copy-done.5, bf16[64,4,128]{2,1,0:T(4,128)(2,1)S(1)} %all-to-all-done.2.back_ref, f32[32,128]{1,0:T(8,128)S(1)} %shard_map.126.base_ref, f32[256,128]{1,0:T(8,128)S(1)} %copy-done.2, bf16[256,32]{1,0:T(8,128)(2,1)S(1)} %copy-done.4), custom_call_target="tpu_custom_call" | custom-call | tf_op jit(solution)/shard_map/pallas_call | solution.py:214
  (10 shorter events, 0.0 us)
Async XLA Ops:
  0.6 36.3 %copy-start = (bf16[1024,512]{1,0:T(8,128)(2,1)S(1)}, bf16[1024,512]{1,0:T(8,128)(2,1)}, u32[]{:S(2)}) copy-start(bf16[1024,512]{1,0:T(8,128)(2,1)} %down_hbm.1) | copy-start | bytes 3145732
  2.9 56.2 %copy-start.3 = (bf16[512,128]{1,0:T(8,128)(2,1)S(1)}, bf16[512,128]{1,0:T(8,128)(2,1)}, u32[]{:S(2)}) copy-start(bf16[512,128]{1,0:T(8,128)(2,1)} %up_hbm.1) | copy-start | bytes 393220
  2.9 34.0 %all-to-all-start = ((bf16[64,4,1152]{2,1,0:T(4,128)(2,1)}), bf16[64,4,1152]{2,1,0:T(4,128)(2,1)S(1)}, u32[]{:S(2)}, u32[]{:S(2)}) async-start(bf16[64,4,1152]{2,1,0:T(4,128)(2,1)} %get-tuple-element.21), calls=%async_computation | async-start | bytes 1179648 | tf_op jit(solution)/shard_map/all_to_all | solution.py:263
  17.9 55.2 %copy-start.1 = (bf16[16,2,1024]{2,1,0:T(2,128)(2,1)S(1)}, bf16[16,2,1024]{2,1,0:T(2,128)(2,1)}, u32[]{:S(2)}) copy-start(bf16[16,2,1024]{2,1,0:T(2,128)(2,1)} %x_ref) | copy-start | bytes 196612
  17.9 9.7 %collective-permute-start = (bf16[16,2,1024]{2,1,0:T(2,128)(2,1)}, bf16[16,2,1024]{2,1,0:T(2,128)(2,1)S(1)}, u32[]{:S(2)}, u32[]{:S(2)}) collective-permute-start(bf16[16,2,1024]{2,1,0:T(2,128)(2,1)} %x_ref), channel_id=1, source_target_pairs={{0,4},{1,5},{2,6},{3,7},{4,0},{5,1},{6,2},{7,3},{8,12},{9,13},{10,... | collective-permute-start | bytes 196616 | tf_op jit(solution)/shard_map/ppermute | solution.py:265
  27.7 7.8 %collective-permute-start.1 = (bf16[32,2,1024]{2,1,0:T(2,128)(2,1)S(1)}, bf16[32,2,1024]{2,1,0:T(2,128)(2,1)S(1)}, u32[]{:S(2)}, u32[]{:S(2)}) collective-permute-start(bf16[32,2,1024]{2,1,0:T(2,128)(2,1)S(1)} %constant_dynamic-update-slice_fusion), channel_id=1, source_target_pairs={{0,3},{1,2},{2,1},{3,0},{4,7},{5,6},{6,5},{7,4},{8,11},{9,10},{10,... | collective-permute-start | bytes 393224 | tf_op jit(solution)/shard_map/ppermute | solution.py:265
  38.6 44.5 %copy-start.2 = (f32[256,128]{1,0:T(8,128)S(1)}, f32[256,128]{1,0:T(8,128)}, u32[]{:S(2)}) copy-start(f32[256,128]{1,0:T(8,128)} %get-tuple-element.36.part_ref) | copy-start | bytes 393220
  38.6 44.5 %copy-start.4 = (bf16[256,32]{1,0:T(8,128)(2,1)S(1)}, bf16[256,32]{1,0:T(8,128)(2,1)}, u32[]{:S(2)}) copy-start(bf16[256,32]{1,0:T(8,128)(2,1)} %get-tuple-element.37.weight_ref) | copy-start | bytes 49156
  38.6 44.5 %copy-start.5 = (s32[16]{0:T(128)S(1)}, s32[16]{0:T(128)}, u32[]{:S(2)}) copy-start(s32[16]{0:T(128)} %get-tuple-element.20.place_ref) | copy-start | bytes 196
  38.7 20.5 %all-to-all-start.1 = ((bf16[8,128,128]{2,1,0:T(8,128)(2,1)}), bf16[8,128,128]{2,1,0:T(8,128)(2,1)S(1)}, u32[]{:S(2)}, u32[]{:S(2)}) async-start(bf16[8,128,128]{2,1,0:T(8,128)(2,1)} %get-tuple-element.28), calls=%async_computation.1 | async-start | bytes 524288 | tf_op jit(solution)/shard_map/all_to_all | solution.py:295
  45.6 8.7 %collective-permute-start.2 = (bf16[32,2,1024]{2,1,0:T(2,128)(2,1)S(1)}, bf16[32,2,1024]{2,1,0:T(2,128)(2,1)S(1)}, u32[]{:S(2)}, u32[]{:S(2)}) collective-permute-start(bf16[32,2,1024]{2,1,0:T(2,128)(2,1)S(1)} %constant_dynamic-update-slice_fusion), channel_id=1, source_target_pairs={{0,1},{1,0},{2,3},{3,2},{4,5},{5,4},{6,7},{7,6},{8,9},{9,8},{10,11... | collective-permute-start | bytes 393224 | tf_op jit(solution)/shard_map/ppermute | solution.py:265
  49.0 10.1 %collective-permute-start.3 = (bf16[32,2,1024]{2,1,0:T(2,128)(2,1)S(1)}, bf16[32,2,1024]{2,1,0:T(2,128)(2,1)S(1)}, u32[]{:S(2)}, u32[]{:S(2)}) collective-permute-start(bf16[32,2,1024]{2,1,0:T(2,128)(2,1)S(1)} %constant_dynamic-update-slice_fusion), channel_id=1, source_target_pairs={{0,2},{1,3},{2,0},{3,1},{4,6},{5,7},{6,4},{7,5},{8,10},{9,11},{10,... | collective-permute-start | bytes 393224 | tf_op jit(solution)/shard_map/ppermute | solution.py:265
  60.5 22.7 %all-to-all-start.2 = ((bf16[64,4,128]{2,1,0:T(4,128)(2,1)}), bf16[64,4,128]{2,1,0:T(4,128)(2,1)S(1)}, u32[]{:S(2)}, u32[]{:S(2)}) async-start(bf16[64,4,128]{2,1,0:T(4,128)(2,1)} %shard_map.125), calls=%async_computation.2 | async-start | bytes 131072 | tf_op jit(solution)/shard_map/all_to_all | solution.py:309

commit v5 on v4

--- a/solution.py
+++ b/solution.py
@@ -26,17 +26,17 @@
     return jnp.dot(a, b, preferred_element_type=F32)
 
 
-def picker(place_ref, rows, steps, requests):
+def picker(place, rows, steps, requests):
     shape = (rows, requests * steps)
     column = iota((1, requests * steps), 1)
     target = jnp.zeros((1, requests * steps), I32)
     for i in range(requests):
-        target = jnp.where(column // steps == i, place_ref[i] * steps + column % steps, target)
+        target = jnp.where(column // steps == i, place[i] * steps + column % steps, target)
     return jnp.where(iota(shape, 0) == target, 1.0, 0.0).astype(BF)
 
 
 def route_kernel(
-    adapters, adapter_hbm, storage_hbm, x_hbm, send_ref, place_ref, adapter_ref, storage_ref, x_ref, sems
+    adapters, adapter_hbm, storage_hbm, x_hbm, send_ref, pick_ref, adapter_ref, storage_ref, x_ref, sems
 ):
     copies = [
         pltpu.make_async_copy(adapter_hbm, adapter_ref, sems.at[0]),
@@ -52,41 +52,32 @@
     copies[1].wait()
     storage = [storage_ref[adapter_ref[i]] for i in range(requests)]
     home = [s // adapters for s in storage]
+    place = []
     code = jnp.zeros((requests * steps, LANES), I32)
     row = iota((requests * steps, LANES), 0)
     for i in range(requests):
         earlier = jnp.int32(0)
         for k in range(i):
             earlier = earlier + (home[k] == home[i]).astype(I32)
-        place_ref[i] = home[i] * CAP + earlier
+        place.append(home[i] * CAP + earlier)
         code = jnp.where(row // steps == i, storage[i] % adapters, code)
-    pick = picker(place_ref, rows, steps, requests)
+    pick = picker(place, rows, steps, requests)
+    pick_ref[...] = pick
     copies[2].wait()
     x = x_ref[...].reshape(requests * steps, width)
     send = dot(pick, jnp.concatenate([x, code.astype(F32).astype(BF)], axis=1))
     send_ref[...] = send.astype(BF).reshape(send_ref.shape)
 
 
-def down_kernel(halves, seen_ref, down_hbm, part_ref, code_hbm, down_ref, code_ref, sems):
+def down_kernel(halves, seen_ref, down_ref, part_ref, code_hbm, code_ref, sem):
     homes, per, width = seen_ref.shape
     width = width - LANES
-    pieces = down_ref.shape[0]
-    deep = width // pieces
-    copies = [
-        pltpu.make_async_copy(down_hbm.at[pl.ds(k * deep, deep)], down_ref.at[k], sems.at[k])
-        for k in range(pieces)
-    ]
-    for copy in copies:
-        copy.start()
     seen = seen_ref[...].reshape(homes * per, width + LANES)
     code = seen[:, width:].astype(F32)
     code_ref[...] = code
-    save = pltpu.make_async_copy(code_ref, code_hbm, sems.at[pieces])
+    save = pltpu.make_async_copy(code_ref, code_hbm, sem)
     save.start()
-    product = jnp.zeros((homes * per, down_ref.shape[2]), F32)
-    for k in range(pieces):
-        copies[k].wait()
-        product = product + dot(seen[:, k * deep : (k + 1) * deep], down_ref[k])
+    product = dot(seen[:, :width], down_ref[...])
     lane = iota(code.shape, 1)
     own = jnp.zeros(code.shape, F32)
     for m in range(product.shape[1] // LANES):
@@ -106,13 +97,9 @@
     save.wait()
 
 
-def up_kernel(halves, part_ref, code_hbm, up_hbm, back_ref, code_ref, up_ref, sems):
-    copies = [
-        pltpu.make_async_copy(code_hbm, code_ref, sems.at[0]),
-        pltpu.make_async_copy(up_hbm, up_ref, sems.at[1]),
-    ]
-    for copy in copies:
-        copy.start()
+def up_kernel(halves, part_ref, code_hbm, up_ref, back_ref, code_ref, sem):
+    load = pltpu.make_async_copy(code_hbm, code_ref, sem)
+    load.start()
     half = code_ref.shape[0] // 2
     total = jnp.zeros((half, LANES), F32)
     for t in range(part_ref.shape[0]):
@@ -124,14 +111,13 @@
     both = jnp.concatenate(
         [jnp.where(left, total, turned), jnp.where(left, turned, total)], axis=0
     )
-    copies[0].wait()
+    load.wait()
     code = code_ref[...]
     lane = iota(code.shape, 1)
     spread = []
     for m in range(up_ref.shape[0] // LANES):
         here = (2 * m + lane // ADAPTER_RANK).astype(F32) == code
         spread.append(jnp.where(here, both, 0.0).astype(BF))
-    copies[1].wait()
     back = dot(jnp.concatenate(spread, axis=1), up_ref[...]).astype(BF)
     back_ref[...] = back.reshape(back_ref.shape)
 
@@ -173,29 +159,33 @@
     part_ref[...] = dot((cached / total).astype(BF), values)
 
 
+def partner(i, d):
+    return ((((i + 1) & 7) ^ 1) + 7) & 7 if d == 3 else i ^ d
+
+
 def base_kernel(index_ref, x_ref, far_ref, *refs):
     value_ref, base_ref = refs[-2:]
     requests, steps, width = x_ref.shape
     rows = requests * steps
     mine = index_ref[0]
-    pieces = [(0, x_ref[...]), (4, far_ref[...])]
+    pieces = [(mine, x_ref[...]), (mine ^ 4, far_ref[...])]
     for k, ref in enumerate(refs[:-2]):
-        pieces.append((k + 1, ref[:requests]))
-        pieces.append((k + 5, ref[requests:]))
+        other = partner(mine, k + 1)
+        pieces.append((other, ref[:requests]))
+        pieces.append((other ^ 4, ref[requests:]))
     total = jnp.zeros(base_ref.shape, F32)
     for other, piece in pieces:
-        start = pl.multiple_of((mine ^ other) * width, width)
+        start = pl.multiple_of(other * width, width)
         total = total + dot(piece.reshape(rows, width), value_ref[pl.ds(start, width), :])
     base_ref[...] = total
 
 
-def finish_kernel(place_ref, back_ref, base_ref, part_ref, weight_ref, step_ref, out_ref):
+def finish_kernel(pick_ref, back_ref, base_ref, part_ref, weight_ref, step_ref, out_ref):
     requests, steps, width = out_ref.shape
     homes, per, columns = back_ref.shape
     n = requests * steps
-    pick = picker(place_ref, homes * per, steps, requests)
     back = back_ref[...].reshape(homes * per, columns)
-    low = lax.dot_general(pick, back, (((0,), (0,)), ((), ())), preferred_element_type=F32)
+    low = lax.dot_general(pick_ref[...], back, (((0,), (0,)), ((), ())), preferred_element_type=F32)
     step = (base_ref[...] + low).astype(BF)
     step_ref[...] = step.reshape(step_ref.shape)
     attended = (part_ref[...] + dot(weight_ref[...], step)).astype(BF)
@@ -247,10 +237,10 @@
     groups = queries.shape[2] // HEAD_WIDTH
     halves = HALVES
     shape = jax.ShapeDtypeStruct
-    send, place = call(
+    send, pick = call(
         functools.partial(route_kernel, A),
         (HB, HB, HB),
-        ((VM, shape((H, CAP * S, W + LANES), BF)), (SM, shape((R,), I32))),
+        ((VM, shape((H, CAP * S, W + LANES), BF)), (VM, shape((rows, R * S), BF))),
         (request_adapter, adapter_storage_row, x),
         (
             pltpu.SMEM(request_adapter.shape, I32),
@@ -262,10 +252,10 @@
     )
     seen = lax.all_to_all(send, "req", 0, 0)
     x, send = lax.optimization_barrier((x, send))
-    swap = lambda v, d: lax.ppermute(v, "tp", [(i, i ^ d) for i in range(T)])
+    swap = lambda v, d: lax.ppermute(v, "tp", [(i, partner(i, d)) for i in range(T)])
     far = swap(x, 4)
     pair = jnp.concatenate([x, far], axis=0)
-    pairs = [swap(pair, d) for d in (3,)]
+    pairs = [swap(pair, d) for d in (2, 1)]
     attended, weights = call(
         scores_kernel,
         (SM, VM, VM, VM, VM),
@@ -275,36 +265,25 @@
         bytes_accessed=10**6,
         mib=60,
     )
-    seen, far, pair, pairs, attended, weights = lax.optimization_barrier(
-        (seen, far, pair, pairs, attended, weights)
-    )
-    pieces = 4
+    seen, far, pair, pairs = lax.optimization_barrier((seen, far, pair, pairs))
     part, code = call(
         functools.partial(down_kernel, halves),
-        (VM, HB),
+        (VM, VM),
         ((VM, shape((T, halves * rows // 2, LANES), BF)), (HB, shape((rows, LANES), F32))),
         (seen, adapter_down_weight),
-        (
-            pltpu.VMEM((pieces, W // pieces, adapter_down_weight.shape[1]), BF),
-            pltpu.VMEM((rows, LANES), F32),
-            pltpu.SemaphoreType.DMA((pieces + 1,)),
-        ),
+        (pltpu.VMEM((rows, LANES), F32), pltpu.SemaphoreType.DMA),
     )
     part, pair = lax.optimization_barrier((part, pair))
-    near = [swap(pair, d) for d in (1, 2)]
+    near = [swap(pair, d) for d in (3,)]
     part = lax.all_to_all(part, "tp", 0, 0)
-    part, near = lax.optimization_barrier((part, near))
-    pairs = near + pairs
+    part, near, attended, weights = lax.optimization_barrier((part, near, attended, weights))
+    pairs = [(pairs + near)[k] for k in (1, 0, 2)]
     (back,) = call(
         functools.partial(up_kernel, halves),
-        (VM, HB, HB),
+        (VM, HB, VM),
         ((VM, shape((H, CAP * S, V), BF)),),
         (part, code, adapter_up_weight),
-        (
-            pltpu.VMEM((rows, LANES), F32),
-            pltpu.VMEM(adapter_up_weight.shape, BF),
-            pltpu.SemaphoreType.DMA((2,)),
-        ),
+        (pltpu.VMEM((rows, LANES), F32), pltpu.SemaphoreType.DMA),
     )
     back = lax.all_to_all(back, "req", 0, 0)
     mine = lax.axis_index("tp").astype(I32).reshape(1)
@@ -318,9 +297,9 @@
     )
     step_values, attention = call(
         finish_kernel,
-        (SM, VM, VM, VM, VM),
+        (VM, VM, VM, VM, VM),
         ((VM, shape((R, S, V), BF)), (VM, shape((R, S, groups * HEAD_WIDTH), BF))),
-        (place, back, base, attended, weights),
+        (pick, back, base, attended, weights),
     )
     return (step_values, attention)
 

time: 85.3 us -> 82.7 us (0.970)
  starting transfers between devices: 54.5 us -> 50.3 us
  waiting for transfers between devices: 16.9 us -> 19.6 us
  Pallas kernels: 11.5 us -> 10.4 us
    ppermute x4, waiting for transfers between devices: 7.49 us -> 11.6 us  [body(): lax.ppermute(v, 'tp', [(i, partner(i, d)) for i in range(T)])]
    all_to_all x1, starting transfers between devices: 6.97 us -> 3.42 us  [body(): part = lax.all_to_all(part, 'tp', 0, 0)]
    all_to_all x1, waiting for transfers between devices: 1.43 us -> 0.01 us  [body(): seen = lax.all_to_all(send, 'req', 0, 0)]
    pallas_call x6, Pallas kernels: 11.5 us -> 10.4 us  [call(): pl.pallas_call(kernel, in_specs=list(ins), out_specs=tuple((s for s, _ in...]
  transfers between devices with their start and end apart: 7 -> 7, of which waited for: 6 -> 5; matrix products, arithmetic and copies ran while one was open for 1% -> 1% of each run, Pallas kernels for 6% -> 6%
where the time goes in v5:
time: 82.7 us; the launch traced here: 82.1 us
  starting transfers between devices  50.3 us (61%)
  waiting for transfers between devices  19.6 us (24%)
  Pallas kernels  10.4 us (13%)
  local copies, waits for them, and re-layouts  0.98 us (1%)
    ppermute x4, starting transfers between devices, body(): lax.ppermute(v, 'tp', [(i, partner(i, d)) for i in range(T)])  20.2 us
    all_to_all x1, starting transfers between devices, body(): seen = lax.all_to_all(send, 'req', 0, 0)  15 us
    all_to_all x1, starting transfers between devices, body(): back = lax.all_to_all(back, 'req', 0, 0)  11.7 us
    ppermute x4, waiting for transfers between devices, body(): lax.ppermute(v, 'tp', [(i, partner(i, d)) for i in range(T)])  11.6 us
    pallas_call x6, Pallas kernels, call(): pl.pallas_call(kernel, in_specs=list(ins), out_specs=tuple((s for s, _ in...  10.4 us
    all_to_all x1, waiting for transfers between devices, body(): back = lax.all_to_all(back, 'req', 0, 0)  8.03 us
    all_to_all x1, starting transfers between devices, body(): part = lax.all_to_all(part, 'tp', 0, 0)  3.42 us
  transfers between devices with their start and end apart: 7, of which 5 were waited for; matrix products, arithmetic and copies ran while one was open for 1% of the time, Pallas kernels for 6%

profile of v5, /device:TPU:1, one launch (start us, length us, event | category | flops | bytes accessed | tf_op | source)
XLA Modules:
  0.0 82.1 jit_solution(2450836641090786020)
XLA Ops:
  0.6 2.2 %shard_map.122 = (bf16[64,4,1152]{2,1,0:T(4,128)(2,1)}, bf16[256,32]{1,0:T(8,128)(2,1)}) custom-call(s32[16]{0:T(128)} %adapter_hbm.1, s32[512]{0:T(512)} %storage_hbm.1, bf16[16,2,1024]{2,1,0:T(2,128)(2,1)} %x_ref), custom_call_target="tpu_custom_call" | custom-call | tf_op jit(solution)/shard_map/pallas_call | solution.py:204
  2.9 0.0 copy-start.3
  2.9 15.0 %all-to-all-start = ((bf16[64,4,1152]{2,1,0:T(4,128)(2,1)}), bf16[64,4,1152]{2,1,0:T(4,128)(2,1)S(1)}, u32[]{:S(2)}, u32[]{:S(2)}) async-start(bf16[64,4,1152]{2,1,0:T(4,128)(2,1)} %get-tuple-element.21), calls=%async_computation | async-start | bytes 1179648 | tf_op jit(solution)/shard_map/all_to_all | solution.py:253
  17.9 0.0 copy-start.1
  17.9 7.6 %collective-permute-start = (bf16[16,2,1024]{2,1,0:T(2,128)(2,1)}, bf16[16,2,1024]{2,1,0:T(2,128)(2,1)S(1)}, u32[]{:S(2)}, u32[]{:S(2)}) collective-permute-start(bf16[16,2,1024]{2,1,0:T(2,128)(2,1)} %x_ref), channel_id=1, source_target_pairs={{0,4},{1,5},{2,6},{3,7},{4,0},{5,1},{6,2},{7,3},{8,12},{9,13},{10,... | collective-permute-start | bytes 196616 | tf_op jit(solution)/shard_map/ppermute | solution.py:255
  25.5 0.9 %constant_dynamic-update-slice_fusion.1 = bf16[32,2,1024]{2,1,0:T(2,128)(2,1)S(1)} fusion(bf16[16,2,1024]{2,1,0:T(2,128)(2,1)} %x_ref), kind=kLoop, calls=%fused_computation.1 | loop fusion | bytes 131072
  26.4 1.2 %collective-permute-done.far_ref = bf16[16,2,1024]{2,1,0:T(2,128)(2,1)S(1)} collective-permute-done((bf16[16,2,1024]{2,1,0:T(2,128)(2,1)}, bf16[16,2,1024]{2,1,0:T(2,128)(2,1)S(1)}, u32[]{:S(2)}, u32[]{:S(2)}) %collective-permute-start) | collective-permute-done | bytes 65568 | tf_op jit(solution)/shard_map/ppermute | solution.py:255
  27.6 0.1 constant_dynamic-update-slice_fusion
  27.7 6.0 %collective-permute-start.1 = (bf16[32,2,1024]{2,1,0:T(2,128)(2,1)S(1)}, bf16[32,2,1024]{2,1,0:T(2,128)(2,1)S(1)}, u32[]{:S(2)}, u32[]{:S(2)}) collective-permute-start(bf16[32,2,1024]{2,1,0:T(2,128)(2,1)S(1)} %constant_dynamic-update-slice_fusion), channel_id=1, source_target_pairs={{0,2},{1,3},{2,0},{3,1},{4,6},{5,7},{6,4},{7,5},{8,10},{9,11},{10,... | collective-permute-start | bytes 393224 | tf_op jit(solution)/shard_map/ppermute | solution.py:255
  33.7 1.9 %collective-permute-start.2 = (bf16[32,2,1024]{2,1,0:T(2,128)(2,1)S(1)}, bf16[32,2,1024]{2,1,0:T(2,128)(2,1)S(1)}, u32[]{:S(2)}, u32[]{:S(2)}) collective-permute-start(bf16[32,2,1024]{2,1,0:T(2,128)(2,1)S(1)} %constant_dynamic-update-slice_fusion), channel_id=1, source_target_pairs={{0,1},{1,0},{2,3},{3,2},{4,5},{5,4},{6,7},{7,6},{8,9},{9,8},{10,11... | collective-permute-start | bytes 393224 | tf_op jit(solution)/shard_map/ppermute | solution.py:255
  35.6 3.7 %collective-permute-done.1.refs_1_ = bf16[32,2,1024]{2,1,0:T(2,128)(2,1)S(1)} collective-permute-done((bf16[32,2,1024]{2,1,0:T(2,128)(2,1)S(1)}, bf16[32,2,1024]{2,1,0:T(2,128)(2,1)S(1)}, u32[]{:S(2)}, u32[]{:S(2)}) %collective-permute-start.1) | collective-permute-done | bytes 131104 | tf_op jit(solution)/shard_map/ppermute | solution.py:255
  39.3 3.0 %collective-permute-done.2.refs_0_ = bf16[32,2,1024]{2,1,0:T(2,128)(2,1)S(1)} collective-permute-done((bf16[32,2,1024]{2,1,0:T(2,128)(2,1)S(1)}, bf16[32,2,1024]{2,1,0:T(2,128)(2,1)S(1)}, u32[]{:S(2)}, u32[]{:S(2)}) %collective-permute-start.2) | collective-permute-done | bytes 131104 | tf_op jit(solution)/shard_map/ppermute | solution.py:255
  42.3 1.4 %shard_map.123 = (bf16[8,128,128]{2,1,0:T(8,128)(2,1)}, f32[256,128]{1,0:T(8,128)S(1)}) custom-call(bf16[64,4,1152]{2,1,0:T(4,128)(2,1)S(1)} %all-to-all-done.seen_ref, bf16[1024,512]{1,0:T(8,128)(2,1)S(1)} %copy-done), custom_call_target="tpu_custom_call" | custom-call | tf_op jit(solution)/shard_map/pallas_call | solution.py:204
  43.8 3.4 %all-to-all-start.1 = ((bf16[8,128,128]{2,1,0:T(8,128)(2,1)}), bf16[8,128,128]{2,1,0:T(8,128)(2,1)S(1)}, u32[]{:S(2)}, u32[]{:S(2)}) async-start(bf16[8,128,128]{2,1,0:T(8,128)(2,1)} %get-tuple-element.26), calls=%async_computation.1 | async-start | bytes 524288 | tf_op jit(solution)/shard_map/all_to_all | solution.py:278
  47.2 0.0 copy-start.4
  47.2 4.6 %collective-permute-start.3 = (bf16[32,2,1024]{2,1,0:T(2,128)(2,1)S(1)}, bf16[32,2,1024]{2,1,0:T(2,128)(2,1)S(1)}, u32[]{:S(2)}, u32[]{:S(2)}) collective-permute-start(bf16[32,2,1024]{2,1,0:T(2,128)(2,1)S(1)} %constant_dynamic-update-slice_fusion), channel_id=1, source_target_pairs={{0,7},{1,2},{2,1},{3,4},{4,3},{5,6},{6,5},{7,0},{8,15},{9,10},{10,... | collective-permute-start | bytes 393224 | tf_op jit(solution)/shard_map/ppermute | solution.py:255
  51.9 2.6 %shard_map.124 = (f32[256,128]{1,0:T(8,128)}, bf16[256,32]{1,0:T(8,128)(2,1)}) custom-call(s32[16]{0:T(128)} %length_ref.1, bf16[16,2,1024]{2,1,0:T(2,128)(2,1)} %q_ref.1, bf16[16,64,128]{2,1,0:T(8,128)(2,1)} %key_ref.1, bf16[16,64,128]{2,1,0:T(8,128)(2,1)} %value_ref.1, bf16[16,2,128]{2,1,0:T(2,128)(2,1)} %fresh_ref.1), custom_call_target="tpu_custom_call" | custom-call | flops 100000000 | bytes 1000000 | tf_op jit(solution)/shard_map/pallas_call | solution.py:204
  54.5 3.7 %collective-permute-done.3.refs_2_ = bf16[32,2,1024]{2,1,0:T(2,128)(2,1)S(1)} collective-permute-done((bf16[32,2,1024]{2,1,0:T(2,128)(2,1)S(1)}, bf16[32,2,1024]{2,1,0:T(2,128)(2,1)S(1)}, u32[]{:S(2)}, u32[]{:S(2)}) %collective-permute-start.3) | collective-permute-done | bytes 131104 | tf_op jit(solution)/shard_map/ppermute | solution.py:255
  58.2 0.0 all-to-all-done.1.part_ref
  58.2 1.1 %shard_map.125 = bf16[64,4,128]{2,1,0:T(4,128)(2,1)} custom-call(bf16[8,128,128]{2,1,0:T(8,128)(2,1)S(1)} %all-to-all-done.1.part_ref, f32[256,128]{1,0:T(8,128)S(1)} %get-tuple-element.31.code_hbm, bf16[512,128]{1,0:T(8,128)(2,1)S(1)} %copy-done.3), custom_call_target="tpu_custom_call" | custom-call | tf_op jit(solution)/shard_map/pallas_call | solution.py:204
  59.3 11.7 %all-to-all-start.2 = ((bf16[64,4,128]{2,1,0:T(4,128)(2,1)}), bf16[64,4,128]{2,1,0:T(4,128)(2,1)S(1)}, u32[]{:S(2)}, u32[]{:S(2)}) async-start(bf16[64,4,128]{2,1,0:T(4,128)(2,1)} %shard_map.125), calls=%async_computation.2 | async-start | bytes 131072 | tf_op jit(solution)/shard_map/all_to_all | solution.py:288
  71.1 2.0 %shard_map.126.base_ref = f32[32,128]{1,0:T(8,128)S(1)} custom-call(s32[1]{0:T(128)} %bitcast.index_ref, bf16[16,2,1024]{2,1,0:T(2,128)(2,1)S(1)} %copy-done.1, bf16[16,2,1024]{2,1,0:T(2,128)(2,1)S(1)} %collective-permute-done.far_ref, bf16[32,2,1024]{2,1,0:T(2,128)(2,1)S(1)} %collective-permute-done.2.refs_0_, ...), custom_call_target="tpu_custom_call" | custom-call | flops 100000000 | tf_op jit(solution)/shard_map/pallas_call | solution.py:204
  73.1 8.0 %all-to-all-done.2.back_ref = bf16[64,4,128]{2,1,0:T(4,128)(2,1)S(1)} async-done(((bf16[64,4,128]{2,1,0:T(4,128)(2,1)}), bf16[64,4,128]{2,1,0:T(4,128)(2,1)S(1)}, u32[]{:S(2)}, u32[]{:S(2)}) %all-to-all-start.2) | async-done | bytes 65568 | tf_op jit(solution)/shard_map/all_to_all | solution.py:288
  81.1 1.0 %shard_map.127 = (bf16[16,2,128]{2,1,0:T(2,128)(2,1)}, bf16[16,2,1024]{2,1,0:T(2,128)(2,1)}) custom-call(bf16[256,32]{1,0:T(8,128)(2,1)S(1)} %copy-done.4, bf16[64,4,128]{2,1,0:T(4,128)(2,1)S(1)} %all-to-all-done.2.back_ref, f32[32,128]{1,0:T(8,128)S(1)} %shard_map.126.base_ref, f32[256,128]{1,0:T(8,128)S(1)} %copy-done.2, bf16[256,32]{1,0:T(8,128)(2,1)S(1)} %copy-done.5), custom_call_target="tpu_custom_call" | custom-call | tf_op jit(solution)/shard_map/pallas_call | solution.py:204
  (10 shorter events, 0.0 us)
Async XLA Ops:
  0.6 41.7 %copy-start = (bf16[1024,512]{1,0:T(8,128)(2,1)S(1)}, bf16[1024,512]{1,0:T(8,128)(2,1)}, u32[]{:S(2)}) copy-start(bf16[1024,512]{1,0:T(8,128)(2,1)} %down_ref.1) | copy-start | bytes 3145732
  2.9 55.3 %copy-start.3 = (bf16[512,128]{1,0:T(8,128)(2,1)S(1)}, bf16[512,128]{1,0:T(8,128)(2,1)}, u32[]{:S(2)}) copy-start(bf16[512,128]{1,0:T(8,128)(2,1)} %up_ref.1) | copy-start | bytes 393220
  2.9 39.4 %all-to-all-start = ((bf16[64,4,1152]{2,1,0:T(4,128)(2,1)}), bf16[64,4,1152]{2,1,0:T(4,128)(2,1)S(1)}, u32[]{:S(2)}, u32[]{:S(2)}) async-start(bf16[64,4,1152]{2,1,0:T(4,128)(2,1)} %get-tuple-element.21), calls=%async_computation | async-start | bytes 1179648 | tf_op jit(solution)/shard_map/all_to_all | solution.py:253
  17.9 53.2 %copy-start.1 = (bf16[16,2,1024]{2,1,0:T(2,128)(2,1)S(1)}, bf16[16,2,1024]{2,1,0:T(2,128)(2,1)}, u32[]{:S(2)}) copy-start(bf16[16,2,1024]{2,1,0:T(2,128)(2,1)} %x_ref) | copy-start | bytes 196612
  17.9 9.7 %collective-permute-start = (bf16[16,2,1024]{2,1,0:T(2,128)(2,1)}, bf16[16,2,1024]{2,1,0:T(2,128)(2,1)S(1)}, u32[]{:S(2)}, u32[]{:S(2)}) collective-permute-start(bf16[16,2,1024]{2,1,0:T(2,128)(2,1)} %x_ref), channel_id=1, source_target_pairs={{0,4},{1,5},{2,6},{3,7},{4,0},{5,1},{6,2},{7,3},{8,12},{9,13},{10,... | collective-permute-start | bytes 196616 | tf_op jit(solution)/shard_map/ppermute | solution.py:255
  27.7 11.6 %collective-permute-start.1 = (bf16[32,2,1024]{2,1,0:T(2,128)(2,1)S(1)}, bf16[32,2,1024]{2,1,0:T(2,128)(2,1)S(1)}, u32[]{:S(2)}, u32[]{:S(2)}) collective-permute-start(bf16[32,2,1024]{2,1,0:T(2,128)(2,1)S(1)} %constant_dynamic-update-slice_fusion), channel_id=1, source_target_pairs={{0,2},{1,3},{2,0},{3,1},{4,6},{5,7},{6,4},{7,5},{8,10},{9,11},{10,... | collective-permute-start | bytes 393224 | tf_op jit(solution)/shard_map/ppermute | solution.py:255
  33.7 8.6 %collective-permute-start.2 = (bf16[32,2,1024]{2,1,0:T(2,128)(2,1)S(1)}, bf16[32,2,1024]{2,1,0:T(2,128)(2,1)S(1)}, u32[]{:S(2)}, u32[]{:S(2)}) collective-permute-start(bf16[32,2,1024]{2,1,0:T(2,128)(2,1)S(1)} %constant_dynamic-update-slice_fusion), channel_id=1, source_target_pairs={{0,1},{1,0},{2,3},{3,2},{4,5},{5,4},{6,7},{7,6},{8,9},{9,8},{10,11... | collective-permute-start | bytes 393224 | tf_op jit(solution)/shard_map/ppermute | solution.py:255
  43.8 14.4 %all-to-all-start.1 = ((bf16[8,128,128]{2,1,0:T(8,128)(2,1)}), bf16[8,128,128]{2,1,0:T(8,128)(2,1)S(1)}, u32[]{:S(2)}, u32[]{:S(2)}) async-start(bf16[8,128,128]{2,1,0:T(8,128)(2,1)} %get-tuple-element.26), calls=%async_computation.1 | async-start | bytes 524288 | tf_op jit(solution)/shard_map/all_to_all | solution.py:278
  47.2 33.9 %copy-start.4 = (bf16[256,32]{1,0:T(8,128)(2,1)S(1)}, bf16[256,32]{1,0:T(8,128)(2,1)}, u32[]{:S(2)}) copy-start(bf16[256,32]{1,0:T(8,128)(2,1)} %get-tuple-element.20.pick_ref) | copy-start | bytes 49156
  47.2 10.9 %collective-permute-start.3 = (bf16[32,2,1024]{2,1,0:T(2,128)(2,1)S(1)}, bf16[32,2,1024]{2,1,0:T(2,128)(2,1)S(1)}, u32[]{:S(2)}, u32[]{:S(2)}) collective-permute-start(bf16[32,2,1024]{2,1,0:T(2,128)(2,1)S(1)} %constant_dynamic-update-slice_fusion), channel_id=1, source_target_pairs={{0,7},{1,2},{2,1},{3,4},{4,3},{5,6},{6,5},{7,0},{8,15},{9,10},{10,... | collective-permute-start | bytes 393224 | tf_op jit(solution)/shard_map/ppermute | solution.py:255
  54.5 26.6 %copy-start.2 = (f32[256,128]{1,0:T(8,128)S(1)}, f32[256,128]{1,0:T(8,128)}, u32[]{:S(2)}) copy-start(f32[256,128]{1,0:T(8,128)} %get-tuple-element.36.part_ref) | copy-start | bytes 393220
  54.5 26.6 %copy-start.5 = (bf16[256,32]{1,0:T(8,128)(2,1)S(1)}, bf16[256,32]{1,0:T(8,128)(2,1)}, u32[]{:S(2)}) copy-start(bf16[256,32]{1,0:T(8,128)(2,1)} %get-tuple-element.37.weight_ref) | copy-start | bytes 49156
  59.3 21.8 %all-to-all-start.2 = ((bf16[64,4,128]{2,1,0:T(4,128)(2,1)}), bf16[64,4,128]{2,1,0:T(4,128)(2,1)S(1)}, u32[]{:S(2)}, u32[]{:S(2)}) async-start(bf16[64,4,128]{2,1,0:T(4,128)(2,1)} %shard_map.125), calls=%async_computation.2 | async-start | bytes 131072 | tf_op jit(solution)/shard_map/all_to_all | solution.py:288

commit v6 on v5

--- a/solution.py
+++ b/solution.py
@@ -29,9 +29,11 @@
 def picker(place, rows, steps, requests):
     shape = (rows, requests * steps)
     column = iota((1, requests * steps), 1)
+    owner = lax.div(column, jnp.int32(steps))
     target = jnp.zeros((1, requests * steps), I32)
     for i in range(requests):
-        target = jnp.where(column // steps == i, place[i] * steps + column % steps, target)
+        target = jnp.where(owner == i, place[i] * steps, target)
+    target = target + lax.rem(column, jnp.int32(steps))
     return jnp.where(iota(shape, 0) == target, 1.0, 0.0).astype(BF)
 
 
@@ -51,16 +53,16 @@
     copies[0].wait()
     copies[1].wait()
     storage = [storage_ref[adapter_ref[i]] for i in range(requests)]
-    home = [s // adapters for s in storage]
+    home = [lax.div(s, jnp.int32(adapters)) for s in storage]
     place = []
     code = jnp.zeros((requests * steps, LANES), I32)
-    row = iota((requests * steps, LANES), 0)
+    owner = lax.div(iota((requests * steps, LANES), 0), jnp.int32(steps))
     for i in range(requests):
         earlier = jnp.int32(0)
         for k in range(i):
             earlier = earlier + (home[k] == home[i]).astype(I32)
         place.append(home[i] * CAP + earlier)
-        code = jnp.where(row // steps == i, storage[i] % adapters, code)
+        code = jnp.where(owner == i, lax.rem(storage[i], jnp.int32(adapters)), code)
     pick = picker(place, rows, steps, requests)
     pick_ref[...] = pick
     copies[2].wait()
@@ -69,14 +71,15 @@
     send_ref[...] = send.astype(BF).reshape(send_ref.shape)
 
 
-def down_kernel(halves, seen_ref, down_ref, part_ref, code_hbm, code_ref, sem):
+def down_kernel(halves, seen_ref, down_ref, part_hbm, code_hbm, part_ref, code_ref, sems):
     homes, per, width = seen_ref.shape
     width = width - LANES
     seen = seen_ref[...].reshape(homes * per, width + LANES)
+    code_ref[...] = seen[:, width:]
+    ranks = part_hbm.shape[0]
+    saves = [pltpu.make_async_copy(code_ref, code_hbm, sems.at[ranks])]
+    saves[0].start()
     code = seen[:, width:].astype(F32)
-    code_ref[...] = code
-    save = pltpu.make_async_copy(code_ref, code_hbm, sem)
-    save.start()
     product = dot(seen[:, :width], down_ref[...])
     lane = iota(code.shape, 1)
     own = jnp.zeros(code.shape, F32)
@@ -91,10 +94,12 @@
         high = part.astype(BF)
         pieces.append(high)
         part = part - high.astype(F32)
-    part = jnp.concatenate(pieces, axis=0)
-    for t in range(part_ref.shape[0]):
-        part_ref[t] = part
-    save.wait()
+    part_ref[...] = jnp.concatenate(pieces, axis=0)
+    for t in range(ranks):
+        saves.append(pltpu.make_async_copy(part_ref, part_hbm.at[t], sems.at[t]))
+        saves[-1].start()
+    for save in saves:
+        save.wait()
 
 
 def up_kernel(halves, part_ref, code_hbm, up_ref, back_ref, code_ref, sem):
@@ -112,7 +117,7 @@
         [jnp.where(left, total, turned), jnp.where(left, turned, total)], axis=0
     )
     load.wait()
-    code = code_ref[...]
+    code = code_ref[...].astype(F32)
     lane = iota(code.shape, 1)
     spread = []
     for m in range(up_ref.shape[0] // LANES):
@@ -269,9 +274,13 @@
     part, code = call(
         functools.partial(down_kernel, halves),
         (VM, VM),
-        ((VM, shape((T, halves * rows // 2, LANES), BF)), (HB, shape((rows, LANES), F32))),
+        ((HB, shape((T, halves * rows // 2, LANES), BF)), (HB, shape((rows, LANES), BF))),
         (seen, adapter_down_weight),
-        (pltpu.VMEM((rows, LANES), F32), pltpu.SemaphoreType.DMA),
+        (
+            pltpu.VMEM((halves * rows // 2, LANES), BF),
+            pltpu.VMEM((rows, LANES), BF),
+            pltpu.SemaphoreType.DMA((T + 1,)),
+        ),
     )
     part, pair = lax.optimization_barrier((part, pair))
     near = [swap(pair, d) for d in (3,)]
@@ -283,7 +292,7 @@
         (VM, HB, VM),
         ((VM, shape((H, CAP * S, V), BF)),),
         (part, code, adapter_up_weight),
-        (pltpu.VMEM((rows, LANES), F32), pltpu.SemaphoreType.DMA),
+        (pltpu.VMEM((rows, LANES), BF), pltpu.SemaphoreType.DMA),
     )
     back = lax.all_to_all(back, "req", 0, 0)
     mine = lax.axis_index("tp").astype(I32).reshape(1)

time: 82.7 us -> 82.6 us (level)
  no operation moved by 1% of the time
where the time goes in v6:
time: 82.6 us; the launch traced here: 82 us
  starting transfers between devices  50.5 us (61%)
  waiting for transfers between devices  19.5 us (24%)
  Pallas kernels  10.3 us (12%)
  local copies, waits for them, and re-layouts  0.98 us (1%)
    ppermute x4, starting transfers between devices, body(): lax.ppermute(v, 'tp', [(i, partner(i, d)) for i in range(T)])  20 us
    all_to_all x1, starting transfers between devices, body(): seen = lax.all_to_all(send, 'req', 0, 0)  15 us
    all_to_all x1, starting transfers between devices, body(): back = lax.all_to_all(back, 'req', 0, 0)  11.9 us
    ppermute x4, waiting for transfers between devices, body(): lax.ppermute(v, 'tp', [(i, partner(i, d)) for i in range(T)])  11.4 us
    pallas_call x6, Pallas kernels, call(): pl.pallas_call(kernel, in_specs=list(ins), out_specs=tuple((s for s, _ in...  10.3 us
    all_to_all x1, waiting for transfers between devices, body(): back = lax.all_to_all(back, 'req', 0, 0)  8.03 us
    all_to_all x1, starting transfers between devices, body(): part = lax.all_to_all(part, 'tp', 0, 0)  3.55 us
  transfers between devices with their start and end apart: 7, of which 5 were waited for; matrix products, arithmetic and copies ran while one was open for 1% of the time, Pallas kernels for 6%

profile of v6, /device:TPU:1, one launch (start us, length us, event | category | flops | bytes accessed | tf_op | source)
XLA Modules:
  0.0 82.0 jit_solution(6373151204742849723)
XLA Ops:
  0.6 2.2 %shard_map.122 = (bf16[64,4,1152]{2,1,0:T(4,128)(2,1)}, bf16[256,32]{1,0:T(8,128)(2,1)}) custom-call(s32[16]{0:T(128)} %adapter_hbm.1, s32[512]{0:T(512)} %storage_hbm.1, bf16[16,2,1024]{2,1,0:T(2,128)(2,1)} %x_ref), custom_call_target="tpu_custom_call" | custom-call | tf_op jit(solution)/shard_map/pallas_call | solution.py:209
  2.8 0.0 copy-start.3
  2.9 15.0 %all-to-all-start = ((bf16[64,4,1152]{2,1,0:T(4,128)(2,1)}), bf16[64,4,1152]{2,1,0:T(4,128)(2,1)S(1)}, u32[]{:S(2)}, u32[]{:S(2)}) async-start(bf16[64,4,1152]{2,1,0:T(4,128)(2,1)} %get-tuple-element.21), calls=%async_computation | async-start | bytes 1179648 | tf_op jit(solution)/shard_map/all_to_all | solution.py:258
  17.8 0.0 copy-start.1
  17.8 7.6 %collective-permute-start = (bf16[16,2,1024]{2,1,0:T(2,128)(2,1)}, bf16[16,2,1024]{2,1,0:T(2,128)(2,1)S(1)}, u32[]{:S(2)}, u32[]{:S(2)}) collective-permute-start(bf16[16,2,1024]{2,1,0:T(2,128)(2,1)} %x_ref), channel_id=1, source_target_pairs={{0,4},{1,5},{2,6},{3,7},{4,0},{5,1},{6,2},{7,3},{8,12},{9,13},{10,... | collective-permute-start | bytes 196616 | tf_op jit(solution)/shard_map/ppermute | solution.py:260
  25.4 0.9 %constant_dynamic-update-slice_fusion.1 = bf16[32,2,1024]{2,1,0:T(2,128)(2,1)S(1)} fusion(bf16[16,2,1024]{2,1,0:T(2,128)(2,1)} %x_ref), kind=kLoop, calls=%fused_computation.1 | loop fusion | bytes 131072
  26.3 1.2 %collective-permute-done.far_ref = bf16[16,2,1024]{2,1,0:T(2,128)(2,1)S(1)} collective-permute-done((bf16[16,2,1024]{2,1,0:T(2,128)(2,1)}, bf16[16,2,1024]{2,1,0:T(2,128)(2,1)S(1)}, u32[]{:S(2)}, u32[]{:S(2)}) %collective-permute-start) | collective-permute-done | bytes 65568 | tf_op jit(solution)/shard_map/ppermute | solution.py:260
  27.6 0.1 constant_dynamic-update-slice_fusion
  27.6 6.0 %collective-permute-start.1 = (bf16[32,2,1024]{2,1,0:T(2,128)(2,1)S(1)}, bf16[32,2,1024]{2,1,0:T(2,128)(2,1)S(1)}, u32[]{:S(2)}, u32[]{:S(2)}) collective-permute-start(bf16[32,2,1024]{2,1,0:T(2,128)(2,1)S(1)} %constant_dynamic-update-slice_fusion), channel_id=1, source_target_pairs={{0,2},{1,3},{2,0},{3,1},{4,6},{5,7},{6,4},{7,5},{8,10},{9,11},{10,... | collective-permute-start | bytes 393224 | tf_op jit(solution)/shard_map/ppermute | solution.py:260
  33.7 1.9 %collective-permute-start.2 = (bf16[32,2,1024]{2,1,0:T(2,128)(2,1)S(1)}, bf16[32,2,1024]{2,1,0:T(2,128)(2,1)S(1)}, u32[]{:S(2)}, u32[]{:S(2)}) collective-permute-start(bf16[32,2,1024]{2,1,0:T(2,128)(2,1)S(1)} %constant_dynamic-update-slice_fusion), channel_id=1, source_target_pairs={{0,1},{1,0},{2,3},{3,2},{4,5},{5,4},{6,7},{7,6},{8,9},{9,8},{10,11... | collective-permute-start | bytes 393224 | tf_op jit(solution)/shard_map/ppermute | solution.py:260
  35.6 3.7 %collective-permute-done.1.refs_1_ = bf16[32,2,1024]{2,1,0:T(2,128)(2,1)S(1)} collective-permute-done((bf16[32,2,1024]{2,1,0:T(2,128)(2,1)S(1)}, bf16[32,2,1024]{2,1,0:T(2,128)(2,1)S(1)}, u32[]{:S(2)}, u32[]{:S(2)}) %collective-permute-start.1) | collective-permute-done | bytes 131104 | tf_op jit(solution)/shard_map/ppermute | solution.py:260
  39.3 3.0 %collective-permute-done.2.refs_0_ = bf16[32,2,1024]{2,1,0:T(2,128)(2,1)S(1)} collective-permute-done((bf16[32,2,1024]{2,1,0:T(2,128)(2,1)S(1)}, bf16[32,2,1024]{2,1,0:T(2,128)(2,1)S(1)}, u32[]{:S(2)}, u32[]{:S(2)}) %collective-permute-start.2) | collective-permute-done | bytes 131104 | tf_op jit(solution)/shard_map/ppermute | solution.py:260
  42.3 0.0 all-to-all-done.seen_ref
  42.3 1.4 %shard_map.123 = (bf16[8,128,128]{2,1,0:T(8,128)(2,1)}, bf16[256,128]{1,0:T(8,128)(2,1)S(1)}) custom-call(bf16[64,4,1152]{2,1,0:T(4,128)(2,1)S(1)} %all-to-all-done.seen_ref, bf16[1024,512]{1,0:T(8,128)(2,1)S(1)} %copy-done), custom_call_target="tpu_custom_call" | custom-call | tf_op jit(solution)/shard_map/pallas_call | solution.py:209
  43.7 0.0 copy-start.4
  43.8 3.6 %all-to-all-start.1 = ((bf16[8,128,128]{2,1,0:T(8,128)(2,1)}), bf16[8,128,128]{2,1,0:T(8,128)(2,1)S(1)}, u32[]{:S(2)}, u32[]{:S(2)}) async-start(bf16[8,128,128]{2,1,0:T(8,128)(2,1)} %get-tuple-element.26), calls=%async_computation.1 | async-start | bytes 524288 | tf_op jit(solution)/shard_map/all_to_all | solution.py:287
  47.3 4.5 %collective-permute-start.3 = (bf16[32,2,1024]{2,1,0:T(2,128)(2,1)S(1)}, bf16[32,2,1024]{2,1,0:T(2,128)(2,1)S(1)}, u32[]{:S(2)}, u32[]{:S(2)}) collective-permute-start(bf16[32,2,1024]{2,1,0:T(2,128)(2,1)S(1)} %constant_dynamic-update-slice_fusion), channel_id=1, source_target_pairs={{0,7},{1,2},{2,1},{3,4},{4,3},{5,6},{6,5},{7,0},{8,15},{9,10},{10,... | collective-permute-start | bytes 393224 | tf_op jit(solution)/shard_map/ppermute | solution.py:260
  51.8 2.6 %shard_map.124 = (f32[256,128]{1,0:T(8,128)}, bf16[256,32]{1,0:T(8,128)(2,1)}) custom-call(s32[16]{0:T(128)} %length_ref.1, bf16[16,2,1024]{2,1,0:T(2,128)(2,1)} %q_ref.1, bf16[16,64,128]{2,1,0:T(8,128)(2,1)} %key_ref.1, bf16[16,64,128]{2,1,0:T(8,128)(2,1)} %value_ref.1, bf16[16,2,128]{2,1,0:T(2,128)(2,1)} %fresh_ref.1), custom_call_target="tpu_custom_call" | custom-call | flops 100000000 | bytes 1000000 | tf_op jit(solution)/shard_map/pallas_call | solution.py:209
  54.5 3.5 %collective-permute-done.3.refs_2_ = bf16[32,2,1024]{2,1,0:T(2,128)(2,1)S(1)} collective-permute-done((bf16[32,2,1024]{2,1,0:T(2,128)(2,1)S(1)}, bf16[32,2,1024]{2,1,0:T(2,128)(2,1)S(1)}, u32[]{:S(2)}, u32[]{:S(2)}) %collective-permute-start.3) | collective-permute-done | bytes 131104 | tf_op jit(solution)/shard_map/ppermute | solution.py:260
  57.9 1.0 %shard_map.125 = bf16[64,4,128]{2,1,0:T(4,128)(2,1)} custom-call(bf16[8,128,128]{2,1,0:T(8,128)(2,1)S(1)} %all-to-all-done.1.part_ref, bf16[256,128]{1,0:T(8,128)(2,1)S(1)} %get-tuple-element.31.code_hbm, bf16[512,128]{1,0:T(8,128)(2,1)S(1)} %copy-done.3), custom_call_target="tpu_custom_call" | custom-call | tf_op jit(solution)/shard_map/pallas_call | solution.py:209
  59.0 11.9 %all-to-all-start.2 = ((bf16[64,4,128]{2,1,0:T(4,128)(2,1)}), bf16[64,4,128]{2,1,0:T(4,128)(2,1)S(1)}, u32[]{:S(2)}, u32[]{:S(2)}) async-start(bf16[64,4,128]{2,1,0:T(4,128)(2,1)} %shard_map.125), calls=%async_computation.2 | async-start | bytes 131072 | tf_op jit(solution)/shard_map/all_to_all | solution.py:297
  70.9 2.0 %shard_map.126.base_ref = f32[32,128]{1,0:T(8,128)S(1)} custom-call(s32[1]{0:T(128)} %bitcast.index_ref, bf16[16,2,1024]{2,1,0:T(2,128)(2,1)S(1)} %copy-done.1, bf16[16,2,1024]{2,1,0:T(2,128)(2,1)S(1)} %collective-permute-done.far_ref, bf16[32,2,1024]{2,1,0:T(2,128)(2,1)S(1)} %collective-permute-done.2.refs_0_, ...), custom_call_target="tpu_custom_call" | custom-call | flops 100000000 | tf_op jit(solution)/shard_map/pallas_call | solution.py:209
  73.0 8.0 %all-to-all-done.2.back_ref = bf16[64,4,128]{2,1,0:T(4,128)(2,1)S(1)} async-done(((bf16[64,4,128]{2,1,0:T(4,128)(2,1)}), bf16[64,4,128]{2,1,0:T(4,128)(2,1)S(1)}, u32[]{:S(2)}, u32[]{:S(2)}) %all-to-all-start.2) | async-done | bytes 65568 | tf_op jit(solution)/shard_map/all_to_all | solution.py:297
  81.0 1.0 %shard_map.127 = (bf16[16,2,128]{2,1,0:T(2,128)(2,1)}, bf16[16,2,1024]{2,1,0:T(2,128)(2,1)}) custom-call(bf16[256,32]{1,0:T(8,128)(2,1)S(1)} %copy-done.4, bf16[64,4,128]{2,1,0:T(4,128)(2,1)S(1)} %all-to-all-done.2.back_ref, f32[32,128]{1,0:T(8,128)S(1)} %shard_map.126.base_ref, f32[256,128]{1,0:T(8,128)S(1)} %copy-done.2, bf16[256,32]{1,0:T(8,128)(2,1)S(1)} %copy-done.5), custom_call_target="tpu_custom_call" | custom-call | tf_op jit(solution)/shard_map/pallas_call | solution.py:209
  (10 shorter events, 0.0 us)
Async XLA Ops:
  0.6 41.7 %copy-start = (bf16[1024,512]{1,0:T(8,128)(2,1)S(1)}, bf16[1024,512]{1,0:T(8,128)(2,1)}, u32[]{:S(2)}) copy-start(bf16[1024,512]{1,0:T(8,128)(2,1)} %down_ref.1) | copy-start | bytes 3145732
  2.8 55.1 %copy-start.3 = (bf16[512,128]{1,0:T(8,128)(2,1)S(1)}, bf16[512,128]{1,0:T(8,128)(2,1)}, u32[]{:S(2)}) copy-start(bf16[512,128]{1,0:T(8,128)(2,1)} %up_ref.1) | copy-start | bytes 393220
  2.9 39.4 %all-to-all-start = ((bf16[64,4,1152]{2,1,0:T(4,128)(2,1)}), bf16[64,4,1152]{2,1,0:T(4,128)(2,1)S(1)}, u32[]{:S(2)}, u32[]{:S(2)}) async-start(bf16[64,4,1152]{2,1,0:T(4,128)(2,1)} %get-tuple-element.21), calls=%async_computation | async-start | bytes 1179648 | tf_op jit(solution)/shard_map/all_to_all | solution.py:258
  17.8 53.1 %copy-start.1 = (bf16[16,2,1024]{2,1,0:T(2,128)(2,1)S(1)}, bf16[16,2,1024]{2,1,0:T(2,128)(2,1)}, u32[]{:S(2)}) copy-start(bf16[16,2,1024]{2,1,0:T(2,128)(2,1)} %x_ref) | copy-start | bytes 196612
  17.8 9.8 %collective-permute-start = (bf16[16,2,1024]{2,1,0:T(2,128)(2,1)}, bf16[16,2,1024]{2,1,0:T(2,128)(2,1)S(1)}, u32[]{:S(2)}, u32[]{:S(2)}) collective-permute-start(bf16[16,2,1024]{2,1,0:T(2,128)(2,1)} %x_ref), channel_id=1, source_target_pairs={{0,4},{1,5},{2,6},{3,7},{4,0},{5,1},{6,2},{7,3},{8,12},{9,13},{10,... | collective-permute-start | bytes 196616 | tf_op jit(solution)/shard_map/ppermute | solution.py:260
  27.6 11.6 %collective-permute-start.1 = (bf16[32,2,1024]{2,1,0:T(2,128)(2,1)S(1)}, bf16[32,2,1024]{2,1,0:T(2,128)(2,1)S(1)}, u32[]{:S(2)}, u32[]{:S(2)}) collective-permute-start(bf16[32,2,1024]{2,1,0:T(2,128)(2,1)S(1)} %constant_dynamic-update-slice_fusion), channel_id=1, source_target_pairs={{0,2},{1,3},{2,0},{3,1},{4,6},{5,7},{6,4},{7,5},{8,10},{9,11},{10,... | collective-permute-start | bytes 393224 | tf_op jit(solution)/shard_map/ppermute | solution.py:260
  33.7 8.6 %collective-permute-start.2 = (bf16[32,2,1024]{2,1,0:T(2,128)(2,1)S(1)}, bf16[32,2,1024]{2,1,0:T(2,128)(2,1)S(1)}, u32[]{:S(2)}, u32[]{:S(2)}) collective-permute-start(bf16[32,2,1024]{2,1,0:T(2,128)(2,1)S(1)} %constant_dynamic-update-slice_fusion), channel_id=1, source_target_pairs={{0,1},{1,0},{2,3},{3,2},{4,5},{5,4},{6,7},{7,6},{8,9},{9,8},{10,11... | collective-permute-start | bytes 393224 | tf_op jit(solution)/shard_map/ppermute | solution.py:260
  43.7 37.3 %copy-start.4 = (bf16[256,32]{1,0:T(8,128)(2,1)S(1)}, bf16[256,32]{1,0:T(8,128)(2,1)}, u32[]{:S(2)}) copy-start(bf16[256,32]{1,0:T(8,128)(2,1)} %get-tuple-element.20.pick_ref) | copy-start | bytes 49156
  43.8 14.2 %all-to-all-start.1 = ((bf16[8,128,128]{2,1,0:T(8,128)(2,1)}), bf16[8,128,128]{2,1,0:T(8,128)(2,1)S(1)}, u32[]{:S(2)}, u32[]{:S(2)}) async-start(bf16[8,128,128]{2,1,0:T(8,128)(2,1)} %get-tuple-element.26), calls=%async_computation.1 | async-start | bytes 524288 | tf_op jit(solution)/shard_map/all_to_all | solution.py:287
  47.3 10.6 %collective-permute-start.3 = (bf16[32,2,1024]{2,1,0:T(2,128)(2,1)S(1)}, bf16[32,2,1024]{2,1,0:T(2,128)(2,1)S(1)}, u32[]{:S(2)}, u32[]{:S(2)}) collective-permute-start(bf16[32,2,1024]{2,1,0:T(2,128)(2,1)S(1)} %constant_dynamic-update-slice_fusion), channel_id=1, source_target_pairs={{0,7},{1,2},{2,1},{3,4},{4,3},{5,6},{6,5},{7,0},{8,15},{9,10},{10,... | collective-permute-start | bytes 393224 | tf_op jit(solution)/shard_map/ppermute | solution.py:260
  54.4 26.6 %copy-start.2 = (f32[256,128]{1,0:T(8,128)S(1)}, f32[256,128]{1,0:T(8,128)}, u32[]{:S(2)}) copy-start(f32[256,128]{1,0:T(8,128)} %get-tuple-element.36.part_ref) | copy-start | bytes 393220
  54.5 26.6 %copy-start.5 = (bf16[256,32]{1,0:T(8,128)(2,1)S(1)}, bf16[256,32]{1,0:T(8,128)(2,1)}, u32[]{:S(2)}) copy-start(bf16[256,32]{1,0:T(8,128)(2,1)} %get-tuple-element.37.weight_ref) | copy-start | bytes 49156
  59.0 22.0 %all-to-all-start.2 = ((bf16[64,4,128]{2,1,0:T(4,128)(2,1)}), bf16[64,4,128]{2,1,0:T(4,128)(2,1)S(1)}, u32[]{:S(2)}, u32[]{:S(2)}) async-start(bf16[64,4,128]{2,1,0:T(4,128)(2,1)} %shard_map.125), calls=%async_computation.2 | async-start | bytes 131072 | tf_op jit(solution)/shard_map/all_to_all | solution.py:297
